TPU v7x, 32 devices: a whole 2x2x4 slice. The times are simulated.
32 devices in a mesh: req: 8 (over z, y), kv: 4 (over x, core).
Axes of the slice: x: 2, y: 2, z: 4, core: 2. Of those that a mesh axis runs over, the one named last changes fastest.
Arguments:
- hidden_in: bfloat16 [8192, 2048], P(('req', 'kv')), may hold values from -6 to 6
- slot_tokens: int32 [8192], replicated, may hold values from 0 to 8191, as said below
- cache_len: int32 [64], P('req'), may hold values from 1 to 2048, 32768 in all
- prefill_start: int32 [8], P('req'), may hold values from 0 to 2048
- key_cache: bfloat16 [64, 2048, 1024], P('req', None, 'kv')
- value_cache: bfloat16 [64, 2048, 1024], P('req', None, 'kv'), may hold values from -18 to 18
- key_prefix: bfloat16 [8, 2048, 1024], P('req', None, 'kv')
- value_prefix: bfloat16 [8, 2048, 1024], P('req', None, 'kv'), may hold values from -18 to 18
- attn_gain: float32 [2048], replicated, may hold values from 0.25 to 1.75
- q_proj: bfloat16 [2048, 2048], P(None, 'kv'), may hold values from -0.125 to 0.125
- k_proj: bfloat16 [2048, 1024], P(None, 'kv'), may hold values from -0.125 to 0.125
- v_proj: bfloat16 [2048, 1024], P(None, 'kv'), may hold values from -0.125 to 0.125
- q_gain: float32 [128], replicated, may hold values from 0.25 to 1.75
- k_gain: float32 [128], replicated, may hold values from 0.25 to 1.75
- o_proj: bfloat16 [2048, 2048], P('kv'), may hold values from -0.125 to 0.125
- ffn_gain: float32 [2048], replicated, may hold values from 0.25 to 1.75
- w_gate: bfloat16 [2048, 6144], P(None, 'req'), may hold values from -0.125 to 0.125
- w_up: bfloat16 [2048, 6144], P(None, 'req'), may hold values from -0.125 to 0.125
- w_down: bfloat16 [6144, 2048], P('req'), may hold values from -0.078125 to 0.078125
- final_gain: float32 [2048], replicated, may hold values from 0.25 to 1.75
- lm_head: bfloat16 [2048, 151936], P(None, ('req', 'kv')), may hold values from -0.375 to 0.375
Outputs:
- layer_out: bfloat16 [8192, 2048], P(('req', 'kv'))
- max_logit: float32 [72], replicated
Inputs may be any that keep to these rules, and one draw needn't show every extreme that they name: slot_tokens is a permutation of the batch's tokens; each device's 256 consecutive slots take exactly 8 tokens from each device's 256 consecutive batch tokens.
All inputs are finite; a program needn't handle non-finite values. No bound on the sum of `cache_len` on one device may be relied on, other than what follows from the above.
Results may differ from a plain program's by a relative error of at most 0.0085.
The roundings to bfloat16 on the way count: a program that leaves them out, or rounds other values in their place, can miss the bound.
Values may be sent and summed in bfloat16 or wider, within the bound.
No kernel may reach another device: no remote copies, remote signals or barrier semaphores. Data moves between devices by JAX's collectives and lax.ppermute only.
A program may use at most 192 MiB of HBM per device.

v0:
```python
import functools
import math

import jax
import jax.numpy as jnp
from jax import lax
from jax.experimental import pallas as pl
from jax.experimental.pallas import tpu as pltpu
from jax.sharding import PartitionSpec as P

EPS = 1e-06
NEG = -1e30
GROUP = 4
TAIL = 16
DECODE_GROUP = 4
KEY_BLOCK = 512
VMEM_LIMIT = 56 * 1024 * 1024
BRIEF = pl.CostEstimate(flops=1, bytes_accessed=1, transcendentals=0)


def swap(value, axis, bit):
    size = lax.axis_size(axis)
    return lax.ppermute(value, axis, [(i, i ^ bit) for i in range(size)])


def bits_below(size):
    return [1 << i for i in range(size.bit_length() - 1)]


def gather_xor(value, axis, bits):
    held = {0: value}
    for bit in bits:
        held.update({diff ^ bit: swap(block, axis, bit) for diff, block in list(held.items())})
    return held


def zero_after(value):
    first = value[(0,) * value.ndim]
    return (first != first).astype(jnp.int32)


def pin(value, *others):
    anywhere = pl.BlockSpec(memory_space=pl.ANY)
    return pl.pallas_call(
        lambda *refs: None,
        out_shape=jax.ShapeDtypeStruct(value.shape, value.dtype),
        in_specs=[anywhere] * (1 + len(others)),
        out_specs=anywhere,
        input_output_aliases={0: 0},
        cost_estimate=BRIEF,
    )(value, *others)


def norm_rows(values, gain_vec):
    wide = values.astype(jnp.float32)
    return wide * lax.rsqrt(jnp.mean(wide * wide, axis=-1, keepdims=True) + EPS) * gain_vec


def angle_tables(places, head_dim):
    half_dim = head_dim // 2
    freqs = 1000000.0 ** (-(jnp.arange(half_dim, dtype=jnp.float32) * 2.0 / head_dim))
    angles = places[:, None] * freqs[None, :]
    return jnp.cos(angles), jnp.sin(angles)


def contract_last(left, right):
    return lax.dot_general(left, right, (((1,), (1,)), ((), ())), preferred_element_type=jnp.float32)


def whole_spec(shape):
    return pl.BlockSpec(shape, lambda *_: (0,) * len(shape))


def project_kernel(block_count, head_dim, *refs):
    row_refs = refs[:block_count]
    (gain_ref, cos_ref, sin_ref, q_gain_ref, k_gain_ref, wq_hbm, wk_hbm, wv_hbm) = refs[
        block_count : block_count + 8
    ]
    q_ref, k_ref, v_ref, wq, wk, wv, sems = refs[-7:]
    copies = [
        pltpu.make_async_copy(hbm, vmem, sems.at[at])
        for at, (hbm, vmem) in enumerate(((wq_hbm, wq), (wk_hbm, wk), (wv_hbm, wv)))
    ]
    for copy in copies:
        copy.start()
    normed = []
    for ref in row_refs:
        wide = ref[...].astype(jnp.float32)
        scale = lax.rsqrt(jnp.mean(wide * wide, axis=-1, keepdims=True) + EPS)
        normed.append((wide * scale * gain_ref[...]).astype(jnp.bfloat16))
    rows = jnp.concatenate(normed, axis=0)
    cosine, sine = cos_ref[...], sin_ref[...]

    def heads(raw, gain, out_ref):
        for at in range(raw.shape[1] // head_dim):
            head = raw[:, at * head_dim : (at + 1) * head_dim]
            scale = lax.rsqrt(jnp.mean(head * head, axis=-1, keepdims=True) + EPS)
            head = head * scale * gain
            turned = head * cosine + pltpu.roll(head, head_dim // 2, 1) * sine
            out_ref[:, at * head_dim : (at + 1) * head_dim] = turned.astype(jnp.bfloat16)

    copies[0].wait()
    heads(matmul(rows, wq[...]), q_gain_ref[...], q_ref)
    copies[1].wait()
    heads(matmul(rows, wk[...]), k_gain_ref[...], k_ref)
    copies[2].wait()
    v_ref[...] = matmul(rows, wv[...]).astype(jnp.bfloat16)


def project(blocks, gain, cosine, sine, q_gain, k_gain, q_proj, k_proj, v_proj):
    head_dim = q_gain.shape[0]
    rows = sum(block.shape[0] for block in blocks)
    width = q_proj.shape[0]
    outs = (q_proj.shape[1], k_proj.shape[1], v_proj.shape[1])
    vectors = (gain[None, :], cosine, sine, q_gain[None, :], k_gain[None, :])
    return pl.pallas_call(
        functools.partial(project_kernel, len(blocks), head_dim),
        out_shape=[jax.ShapeDtypeStruct((rows, cols), jnp.bfloat16) for cols in outs],
        in_specs=[whole_spec(block.shape) for block in blocks]
        + [whole_spec(vector.shape) for vector in vectors]
        + [pl.BlockSpec(memory_space=pl.ANY)] * 3,
        out_specs=[whole_spec((rows, cols)) for cols in outs],
        grid=(1,),
        scratch_shapes=[pltpu.VMEM((width, cols), jnp.bfloat16) for cols in outs]
        + [pltpu.SemaphoreType.DMA((3,))],
        compiler_params=pltpu.CompilerParams(vmem_limit_bytes=VMEM_LIMIT),
        cost_estimate=BRIEF,
    )(*blocks, *vectors, q_proj, k_proj, v_proj)


def share_kernel(share, tile, index_ref, gate, up, down, _, out, sems):
    at = pl.ds(pl.multiple_of(index_ref[0] * share, share), share)
    hidden = gate.shape[1]
    copies = [(gate.at[at, :], out.at[pl.ds(0, share), pl.ds(0, hidden)])]
    copies.append((up.at[at, :], out.at[pl.ds(0, share), pl.ds(hidden, hidden)]))
    for step in range(hidden // tile):
        rows, lanes = pl.ds(step * tile, tile), pl.ds(step * share, share)
        copies.append((down.at[rows, at], out.at[pl.ds(share, tile), lanes]))
    copies = [pltpu.make_async_copy(*ends, sems.at[at]) for at, ends in enumerate(copies)]
    for copy in copies:
        copy.start()
    for copy in copies:
        copy.wait()


def share_of(index, share, gate, up, down, follows):
    hidden = gate.shape[1]
    tile = share // 2
    return pl.pallas_call(
        functools.partial(share_kernel, share, tile),
        out_shape=jax.ShapeDtypeStruct((share + tile, 2 * hidden), gate.dtype),
        in_specs=[pl.BlockSpec(memory_space=pltpu.SMEM)] + [pl.BlockSpec(memory_space=pl.ANY)] * 4,
        out_specs=pl.BlockSpec(memory_space=pl.ANY),
        scratch_shapes=[pltpu.SemaphoreType.DMA((2 + hidden // tile,))],
        cost_estimate=BRIEF,
    )(index, gate, up, down, follows)


def attend_kernel(pair, block_count, head_dim, lens_ref, *refs):
    q_refs, refs = refs[:2], refs[2:]
    k_refs, refs = refs[:block_count], refs[block_count:]
    v_refs, refs = refs[:block_count], refs[block_count:]
    sources, refs = refs[:3], refs[3 + 1 :]
    even_ref, odd_ref, last_ref, k_all, v_all, peak, acc, attended, kp, vp, weight, sems = refs
    copies = [
        pltpu.make_async_copy(source, target, sems.at[at])
        for at, (source, target) in enumerate(zip(sources, (kp, vp, weight)))
    ]
    for copy in copies:
        copy.start()
    kv_index, start = lens_ref[0], lens_ref[1]
    rows, q_cols = q_refs[0].shape
    kv_cols = k_all.shape[1]
    group = q_cols // kv_cols
    heads = q_cols // head_dim
    span = 2 * rows
    scale = head_dim**-0.5 * math.log2(math.e)
    for refs, whole in ((k_refs, k_all), (v_refs, v_all)):
        for at, ref in enumerate(refs):
            whole[at * rows : (at + 1) * rows, :] = ref[...]
    queries = [
        jnp.concatenate([ref[:, head * head_dim : (head + 1) * head_dim] for ref in q_refs], axis=0)
        for head in range(heads)
    ]
    peak[...] = jnp.full(peak.shape, NEG, jnp.float32)
    acc[...] = jnp.zeros(acc.shape, jnp.float32)

    def absorb(keys_ref, values_ref, place, size, allowed):
        for head in range(heads):
            lanes = slice(head // group * head_dim, (head // group + 1) * head_dim)
            keys = keys_ref[pl.ds(place, size), lanes]
            values = values_ref[pl.ds(place, size), lanes]
            wide = jnp.concatenate([values, jnp.ones_like(values)], axis=1)
            scores = contract_last(queries[head], keys)
            if allowed is not None:
                scores = jnp.where(allowed, scores, NEG)
            old = peak[head][:, :1]
            new = jnp.maximum(old, jnp.max(scores, axis=1, keepdims=True))
            weights = jnp.exp2((scores - new) * scale).astype(jnp.bfloat16)
            acc[head] = acc[head] * jnp.exp2((old - new) * scale) + matmul(weights, wide)
            peak[head] = jnp.broadcast_to(new, peak.shape[1:])

    turned = kv_index % 2

    def order(axis):
        ids = lax.broadcasted_iota(jnp.int32, (span, span), axis)
        swapped = jnp.where(ids < rows, ids + rows, ids - rows)
        return jnp.where(turned == 1, swapped, ids)

    absorb(k_all, v_all, pair * span, span, order(1) <= order(0))

    def fresh_block(at, carry):
        @pl.when(((kv_index // 2) ^ at) < ((kv_index // 2) ^ pair))
        def _():
            absorb(k_all, v_all, pl.multiple_of(at * span, span), span, None)

        return carry

    lax.fori_loop(0, block_count // 2, fresh_block, 0)
    copies[0].wait()
    copies[1].wait()
    full = start // KEY_BLOCK

    def prefix_block(at, carry):
        absorb(kp, vp, pl.multiple_of(at * KEY_BLOCK, KEY_BLOCK), KEY_BLOCK, None)
        return carry

    lax.fori_loop(0, full, prefix_block, 0)

    @pl.when(full * KEY_BLOCK < start)
    def _():
        place = pl.multiple_of(full * KEY_BLOCK, KEY_BLOCK)
        ids = lax.broadcasted_iota(jnp.int32, (span, KEY_BLOCK), 1)
        absorb(kp, vp, place, KEY_BLOCK, ids < start - place)

    for head in range(heads):
        attended[:, head * head_dim : (head + 1) * head_dim] = (
            acc[head][:, :head_dim] / acc[head][:, head_dim:]
        ).astype(jnp.bfloat16)
    copies[2].wait()
    width = weight.shape[1]
    for at in range(0, width, q_cols):
        part = matmul(attended[...], weight[:, at : at + q_cols])
        even_ref[:, at : at + q_cols] = part[:rows].astype(even_ref.dtype)
        odd_ref[:, at : at + q_cols] = part[rows:].astype(odd_ref.dtype)
    last = kv_index ^ (block_count - 1)
    here = pl.multiple_of((last % 2) * rows + rows - TAIL, TAIL)
    last_ref[:, :q_cols] = attended[pl.ds(here, TAIL), :]
    ends = [ref[rows - TAIL :, :] for ref in q_refs]
    last_ref[:, q_cols : 2 * q_cols] = jnp.where(last % 2 == 1, ends[1], ends[0])
    there = pl.ds(pl.multiple_of(last * rows + rows - TAIL, TAIL), TAIL)
    last_ref[:, 2 * q_cols : 2 * q_cols + kv_cols] = k_all[there, :]
    last_ref[:, 2 * q_cols + kv_cols :] = v_all[there, :]


def attend(pair, lens, parts, head_dim, key_prefix, value_prefix, o_proj, even_type, follows):
    block_count = len(parts)
    queries, keys, values = [[part[at] for part in parts] for at in range(3)]
    queries = queries[2 * pair : 2 * pair + 2]
    rows, q_cols = queries[0].shape
    kv_cols = keys[0].shape[1]
    width = o_proj.shape[1]
    heads = q_cols // head_dim
    outs = [
        jax.ShapeDtypeStruct((rows, width), even_type),
        jax.ShapeDtypeStruct((rows, width), jnp.bfloat16),
        jax.ShapeDtypeStruct((TAIL, 2 * q_cols + 2 * kv_cols), jnp.bfloat16),
    ]
    return pl.pallas_call(
        functools.partial(attend_kernel, pair, block_count, head_dim),
        out_shape=outs,
        grid_spec=pltpu.PrefetchScalarGridSpec(
            num_scalar_prefetch=1,
            grid=(1,),
            in_specs=[whole_spec(part.shape) for part in queries + keys + values]
            + [pl.BlockSpec(memory_space=pl.ANY)] * 4,
            out_specs=[whole_spec(out.shape) for out in outs],
            scratch_shapes=[
                pltpu.VMEM((rows * block_count, kv_cols), jnp.bfloat16),
                pltpu.VMEM((rows * block_count, kv_cols), jnp.bfloat16),
                pltpu.VMEM((heads, 2 * rows, head_dim), jnp.float32),
                pltpu.VMEM((heads, 2 * rows, 2 * head_dim), jnp.float32),
                pltpu.VMEM((2 * rows, q_cols), jnp.bfloat16),
                pltpu.VMEM(key_prefix.shape, jnp.bfloat16),
                pltpu.VMEM(value_prefix.shape, jnp.bfloat16),
                pltpu.VMEM(o_proj.shape, jnp.bfloat16),
                pltpu.SemaphoreType.DMA((3,)),
            ],
        ),
        compiler_params=pltpu.CompilerParams(vmem_limit_bytes=VMEM_LIMIT),
        cost_estimate=BRIEF,
    )(lens, *queries, *keys, *values, key_prefix, value_prefix, o_proj, follows)


def decode_kernel(pairs, block_count, head_dim, q_cols, kv_cols, lens_ref, *refs):
    last_refs, refs = refs[:pairs], refs[pairs:]
    o_hbm, kc_hbm, vc_hbm, out_ref, kc, vc, weight, dec_in, dec_out, sems, weight_sem = refs
    kv_index = lens_ref[0]
    dec_count, slots = kc.shape[:2]
    group = q_cols // kv_cols
    kv_heads = kv_cols // head_dim
    heads = q_cols // head_dim
    scale = head_dim**-0.5 * math.log2(math.e)
    sizes = (slots // 4, slots // 2, slots)

    def by_size(together, act):
        first = together * DECODE_GROUP
        length = lens_ref[2 + first]
        for at in range(1, DECODE_GROUP):
            length = jnp.maximum(length, lens_ref[2 + first + at])
        for at, size in enumerate(sizes):
            fits = length <= size
            if at:
                fits = fits & (length > sizes[at - 1])
            pl.when(fits)(functools.partial(act, first, size))

    def cache_copies(request, size):
        return (
            pltpu.make_async_copy(
                kc_hbm.at[request, pl.ds(0, size)], kc.at[request, pl.ds(0, size)], sems.at[0, request]
            ),
            pltpu.make_async_copy(
                vc_hbm.at[request, pl.ds(0, size)], vc.at[request, pl.ds(0, size)], sems.at[1, request]
            ),
        )

    def start_copies(first, size):
        for at in range(DECODE_GROUP):
            for copy in cache_copies(first + at, size):
                copy.start()

    for together in range(dec_count // DECODE_GROUP):
        by_size(together, start_copies)
    weight_copy = pltpu.make_async_copy(o_hbm, weight, weight_sem)
    weight_copy.start()
    held = last_refs[0][...]
    for at in range(1, pairs):
        held = jnp.where((kv_index ^ (block_count - 1)) // 2 == at, last_refs[at][...], held)
    rows_in = held[TAIL - dec_count :, q_cols:].astype(jnp.float32)
    for request in range(dec_count):
        dec_in[request] = rows_in[request : request + 1]

    def attend_some(first, size):
        for at in range(DECODE_GROUP):
            attend_one(first + at, size)

    def attend_one(request, size):
        for copy in cache_copies(request, size):
            copy.wait()
        row = dec_in[request]
        empty = jnp.zeros((1, head_dim), jnp.float32)
        spread = []
        for at in range(heads):
            parts = [empty] * kv_heads
            parts[at // group] = row[:, at * head_dim : (at + 1) * head_dim]
            spread.append(jnp.concatenate(parts, axis=1))
        spread += [jnp.zeros((1, kv_cols), jnp.float32)] * (8 - len(spread))
        q_rows = jnp.concatenate(spread, axis=0)
        key_self = row[:, q_cols : q_cols + kv_cols]
        value_self = row[:, q_cols + kv_cols :]
        past = contract_last(q_rows.astype(jnp.bfloat16), kc[request, :size, :])
        ids = lax.broadcasted_iota(jnp.int32, past.shape, 1)
        past = jnp.where(ids < lens_ref[2 + request], past, NEG)
        own = jnp.sum(q_rows * key_self, axis=1, keepdims=True)
        top = jnp.maximum(jnp.max(past, axis=1, keepdims=True), own)
        past = jnp.exp2((past - top) * scale)
        own = jnp.exp2((own - top) * scale)
        total = jnp.sum(past, axis=1, keepdims=True) + own
        past = (past / total).astype(jnp.bfloat16)
        own = (own / total).astype(jnp.bfloat16).astype(jnp.float32)
        summed = matmul(past, vc[request, :size, :]) + own * value_self
        outs = []
        for at in range(heads):
            lane = (at // group) * head_dim
            outs.append(summed[at : at + 1, lane : lane + head_dim])
        dec_out[request] = jnp.concatenate(outs, axis=1)

    for together in range(dec_count // DECODE_GROUP):
        by_size(together, attend_some)
    done = [dec_out[request] for request in range(dec_count)]
    rows = jnp.concatenate([held[: TAIL - dec_count, :q_cols].astype(jnp.float32)] + done, axis=0)
    weight_copy.wait()
    out_ref[...] = matmul(rows.astype(jnp.bfloat16), weight[...]).astype(jnp.bfloat16)


def decode(lens, lasts, head_dim, block_count, o_proj, key_cache, value_cache, follows):
    dec_count, slots, kv_cols = key_cache.shape
    q_cols, width = o_proj.shape
    pairs = len(lasts)

    def kernel(lens_ref, *refs):
        given = pairs + 3
        decode_kernel(
            pairs, block_count, head_dim, q_cols, kv_cols, lens_ref, *refs[:given], *refs[given + 1 :]
        )

    return pl.pallas_call(
        kernel,
        out_shape=jax.ShapeDtypeStruct((TAIL, width), jnp.bfloat16),
        grid_spec=pltpu.PrefetchScalarGridSpec(
            num_scalar_prefetch=1,
            grid=(1,),
            in_specs=[whole_spec(last.shape) for last in lasts]
            + [pl.BlockSpec(memory_space=pl.ANY)] * 4,
            out_specs=whole_spec((TAIL, width)),
            scratch_shapes=[
                pltpu.VMEM((dec_count, slots, kv_cols), jnp.bfloat16),
                pltpu.VMEM((dec_count, slots, kv_cols), jnp.bfloat16),
                pltpu.VMEM(o_proj.shape, jnp.bfloat16),
                pltpu.VMEM((dec_count, 1, q_cols + 2 * kv_cols), jnp.float32),
                pltpu.VMEM((dec_count, 1, q_cols), jnp.float32),
                pltpu.SemaphoreType.DMA((2, dec_count)),
                pltpu.SemaphoreType.DMA,
            ],
        ),
        compiler_params=pltpu.CompilerParams(vmem_limit_bytes=VMEM_LIMIT),
        cost_estimate=BRIEF,
    )(lens, *lasts, o_proj, key_cache, value_cache, follows)


def feed_kernel(tiles, counts, added, *refs):
    pieces = len(counts)
    x_refs, refs = refs[:pieces], refs[pieces:]
    add_refs, refs = refs[:added], refs[added:]
    weight_refs, refs = refs[: len(refs) - 2 - pieces], refs[len(refs) - 2 - pieces :]
    out_refs, (x_all, total) = refs[:pieces], refs[pieces:]
    step = pl.program_id(0)
    cuts = [sum(counts[:at]) for at in range(pieces + 1)]

    @pl.when(step == 0)
    def _():
        for at, ref in enumerate(x_refs):
            x_all[cuts[at] : cuts[at + 1], :] = ref[...]
        for at, ref in enumerate(add_refs):
            total[cuts[at] : cuts[at + 1], :] = ref[...]

    sets = len(weight_refs) // 3
    for at in range(sets):
        gate_ref, up_ref, down_ref = weight_refs[3 * at : 3 * at + 3]

        @pl.when(step // tiles == at)
        def _():
            rows = x_all[...]
            tile = gate_ref.shape[-1]
            gate = matmul(rows, gate_ref[...].reshape(-1, tile))
            up = matmul(rows, up_ref[...].reshape(-1, tile))
            act = (gate / (1.0 + jnp.exp(-gate)) * up).astype(jnp.bfloat16)
            if len(down_ref.shape) == 2:
                downs = [down_ref[...]]
            else:
                downs = [down_ref[part] for part in range(down_ref.shape[0])]
            lane = 0
            for down in downs:
                lanes = slice(lane, lane + down.shape[1])
                lane += down.shape[1]
                part = matmul(act, down)
                if at or added:
                    total[:, lanes] += part
                else:
                    total[:, lanes] = jnp.where(step == 0, part, total[:, lanes] + part)

    @pl.when(step == sets * tiles - 1)
    def _():
        for at, ref in enumerate(out_refs):
            ref[...] = total[cuts[at] : cuts[at + 1], :].astype(ref.dtype)


def feed_forward(blocks, dtypes, weights, follows, adds=()):
    counts = [block.shape[0] for block in blocks]
    size, width = sum(counts), blocks[0].shape[1]
    held = weights[0]
    hidden = held[0].shape[1] if isinstance(held, tuple) else held.shape[2] // 2
    tile = 256 if hidden % 256 == 0 else 128
    tiles = hidden // tile
    specs, operands = [], []
    for at, held in enumerate(weights):

        def place(step, at=at):
            return jnp.clip(step - at * tiles, 0, tiles - 1)

        if isinstance(held, tuple):
            specs += [
                pl.BlockSpec((width, tile), lambda step, place=place: (0, place(step))),
                pl.BlockSpec((width, tile), lambda step, place=place: (0, place(step))),
                pl.BlockSpec((tile, width), lambda step, place=place: (place(step), 0)),
            ]
            operands += held
            continue
        shares = held.shape[0]
        share = width // shares
        specs += [
            pl.BlockSpec((shares, share, tile), lambda step, place=place: (0, 0, place(step))),
            pl.BlockSpec((shares, share, tile), lambda step, place=place: (0, 0, tiles + place(step))),
            pl.BlockSpec(
                (shares, tile, share),
                lambda step, place=place, below=share // tile: (0, below, place(step)),
            ),
        ]
        operands += [held] * 3

    def kernel(*refs):
        given = len(blocks) + len(adds) + len(operands)
        feed_kernel(tiles, counts, len(adds), *refs[:given], *refs[given + len(follows) :])

    return pl.pallas_call(
        kernel,
        out_shape=[
            jax.ShapeDtypeStruct((count, width), dtype) for count, dtype in zip(counts, dtypes)
        ],
        grid=(len(weights) * tiles,),
        in_specs=[whole_spec(block.shape) for block in blocks]
        + [whole_spec(add.shape) for add in adds]
        + specs
        + [pl.BlockSpec(memory_space=pl.ANY)] * len(follows),
        out_specs=[whole_spec((count, width)) for count in counts],
        scratch_shapes=[
            pltpu.VMEM((size, width), jnp.bfloat16),
            pltpu.VMEM((size, width), jnp.float32),
        ],
        compiler_params=pltpu.CompilerParams(vmem_limit_bytes=VMEM_LIMIT),
        cost_estimate=BRIEF,
    )(*blocks, *adds, *operands, *follows)


def regroup(rows_in):
    return lax.all_to_all(rows_in, ("req", "kv"), split_axis=0, concat_axis=0, tiled=True)


def matmul(left, right):
    return jnp.dot(left, right, preferred_element_type=jnp.float32)


def routes(slot_tokens, self_index, devices, rows_dev, ready):
    per_pair = rows_dev // devices
    slot_table = slot_tokens.reshape(devices, rows_dev)
    source = slot_table // rows_dev
    places = jnp.arange(rows_dev, dtype=jnp.int32)
    before = (places[:, None] < places[None, :]).astype(jnp.bfloat16)
    from_self = source == self_index
    rank = matmul(from_self.astype(jnp.bfloat16), before).astype(jnp.int32)
    local = slot_table - self_index * rows_dev
    ranked = jnp.where(from_self, rank, -1)[:, None, :] == jnp.arange(per_pair, dtype=jnp.int32)[None, :, None]
    send_rows = jnp.sum(jnp.where(ranked, local[:, None, :], 0), axis=2).reshape(-1)
    send_hot = (send_rows[:, None] == places[None, :]).astype(jnp.bfloat16)
    own = lax.dynamic_index_in_dim(source, self_index, 0, keepdims=False)
    earlier = (own[:, None] == own[None, :]) & (places[:, None] > places[None, :])
    own_rank = jnp.sum(earlier.astype(jnp.int32), axis=1)
    slot_hot = ((own * per_pair + own_rank + ready)[:, None] == places[None, :]).astype(jnp.bfloat16)
    return send_hot, slot_hot


def pick(hot, rows, transposed=False):
    if transposed:
        return lax.dot_general(
            hot, rows, (((0,), (0,)), ((), ())), preferred_element_type=jnp.float32
        ).astype(rows.dtype)
    return matmul(hot, rows).astype(rows.dtype)


def shards(
    hidden_in,
    slot_tokens,
    cache_len,
    prefill_start,
    key_cache,
    value_cache,
    key_prefix,
    value_prefix,
    attn_gain,
    q_proj,
    k_proj,
    v_proj,
    q_gain,
    k_gain,
    o_proj,
    ffn_gain,
    w_gate,
    w_up,
    w_down,
    final_gain,
    lm_head,
):
    req_count = lax.axis_size("req")
    kv_count = lax.axis_size("kv")
    devices = req_count * kv_count
    rows_dev, width = hidden_in.shape
    kv_index = lax.axis_index("kv")
    self_index = lax.axis_index("req") * kv_count + kv_index
    kv_bits = bits_below(kv_count)
    near_bits = [bit for bit in bits_below(req_count) if bit < GROUP]

    head_dim = q_gain.shape[0]
    dec_count = cache_len.shape[0]
    tok_req = rows_dev * kv_count
    fresh_count = tok_req - dec_count
    places = jnp.concatenate(
        [prefill_start[0] + jnp.arange(fresh_count, dtype=jnp.int32), cache_len]
    ).astype(jnp.float32)
    cosines, sines = angle_tables(places, head_dim)
    cosines = jnp.concatenate([cosines, cosines], axis=1)
    sines = jnp.concatenate([-sines, sines], axis=1)

    cosines, sines = lax.optimization_barrier((cosines, sines))
    ready = sum(zero_after(each) for each in (cosines, sines))

    send_hot, slot_hot = routes(slot_tokens, self_index, devices, rows_dev, ready)
    sent = pick(send_hot, hidden_in)
    far_count = req_count // GROUP
    far_share = share_of(kv_index[None], width // kv_count, w_gate, w_up, w_down, sent)
    step = GROUP if far_count > 2 else GROUP // 2
    ring = [(i, (i + step) % req_count) for i in range(req_count)]
    far_shares = [far_share]
    for _ in range(max(2, far_count - 1)):
        far_shares.append(lax.ppermute(far_shares[-1], "req", ring))
    far_shares = far_shares[GROUP // step :]
    arrived = regroup(sent)
    owner_rows = pick(slot_hot, arrived)

    def project_block(diff):
        block_at = (kv_index ^ diff) * rows_dev
        tables = [lax.dynamic_slice_in_dim(table, block_at, rows_dev, 0) for table in (cosines, sines)]
        return project([blocks[diff]], attn_gain, *tables, q_gain, k_gain, q_proj, k_proj, v_proj)

    even = gather_xor(owner_rows, "kv", kv_bits[:0:-1])
    blocks = {0: owner_rows, 1: swap(owner_rows, "kv", 1)}
    parts = [project_block(0), project_block(1)]
    for diff in range(2, kv_count, 2):
        blocks[diff] = pin(even[diff], parts[1][2])
        blocks[diff + 1] = swap(blocks[diff], "kv", 1)
    for diff in range(2, kv_count):
        parts.append(project_block(diff))

    f32, bf16 = jnp.float32, jnp.bfloat16
    lens = jnp.concatenate([kv_index[None], prefill_start, cache_len]).astype(jnp.int32)
    follows, lasts, sums = parts[-1][2], {}, []
    for pair in range(kv_count // 2 - 1, -1, -1):
        sum_even, sum_odd, lasts[pair] = attend(
            pair,
            lens,
            parts,
            head_dim,
            key_prefix[0],
            value_prefix[0],
            o_proj,
            bf16 if pair else f32,
            follows,
        )
        if pair:
            both = sum_even.astype(f32) + swap(sum_odd, "kv", 1).astype(f32)
            follows = both.astype(bf16)
            sums.append(swap(follows, "kv", 2 * pair))
        else:
            sums.append(swap(pin(sum_odd, *sums), "kv", 1))
            own_sum = sum_even
    far_weights = [
        lax.all_gather(pin(held, own_sum, *sums[:-1]), "kv") for held in far_shares
    ]
    resid = owner_rows.astype(f32) + own_sum
    for each in sums:
        resid = resid + each.astype(f32)
    resid = resid.astype(bf16)
    ffn_in = norm_rows(resid, ffn_gain).astype(bf16)

    own_weights = (w_gate, w_up, w_down)
    near = {0: ffn_in, 1: swap(ffn_in, "req", 1), 2: swap(ffn_in, "req", 2)}

    last_sum = decode(
        lens,
        [lasts[pair] for pair in range(kv_count // 2)],
        head_dim,
        kv_count,
        o_proj,
        key_cache,
        value_cache,
        ffn_in,
    )
    last_raw = blocks[0][rows_dev - TAIL :]
    for diff in range(1, kv_count):
        is_last = (kv_index ^ diff) == kv_count - 1
        last_raw = jnp.where(is_last, blocks[diff][rows_dev - TAIL :], last_raw)
    last_resid = last_raw.astype(f32) + last_sum.astype(f32)
    for diff in range(1, kv_count):
        last_resid = last_resid + swap(last_sum, "kv", diff).astype(f32)
    last_resid = last_resid.astype(bf16)
    last_in = norm_rows(last_resid, ffn_gain).astype(bf16)

    last_near = gather_xor(last_in, "req", near_bits)
    lasts_in = [last_near[diff] for diff in range(GROUP)]

    zero = feed_forward([ffn_in], [f32], [own_weights], [last_sum])
    near[3] = swap(near[1], "req", 2)
    some = feed_forward([near[1], near[2]], [f32] * 2, [own_weights], [zero[0], *lasts_in])
    rest = feed_forward([near[3], *lasts_in], [f32] * (1 + GROUP), [own_weights], some[:1])
    first, second = feed_forward([near[1], near[2]], [bf16] * 2, far_weights, rest[:1], some)
    third, last_part, *last_parts = feed_forward(
        [near[3], *lasts_in], [bf16, f32] + [bf16] * (GROUP - 1), far_weights, [first], rest
    )
    backs = [swap(first, "req", 1), swap(second, "req", 2), swap(third, "req", 3)]
    (own_part,) = feed_forward([ffn_in], [f32], far_weights, [third, *backs[:2]], zero)
    for diff, part in enumerate(last_parts, 1):
        last_part = last_part + swap(part, "req", diff).astype(f32)
    last_rows = (last_resid.astype(f32) + last_part).astype(bf16)
    ffn_part = own_part
    for back in backs:
        ffn_part = ffn_part + back.astype(f32)
    out_rows = (resid.astype(f32) + ffn_part).astype(bf16)
    ends = jnp.where(kv_index == kv_count - 1, last_rows, out_rows[rows_dev - TAIL :])
    out_rows = jnp.concatenate([out_rows[: rows_dev - TAIL], ends], axis=0)
    returned = regroup(pick(slot_hot, out_rows, transposed=True))
    layer_out = pick(send_hot, returned, transposed=True)

    tail_count = dec_count + 1
    tails = pin(norm_rows(last_rows, final_gain).astype(bf16), own_part)
    req_bits = bits_below(req_count)
    for bit in req_bits:
        if bit == req_bits[-1]:
            tails = pin(tails, out_rows)
        tails = jnp.concatenate([tails, swap(tails, "req", bit)], axis=0)
    peaks = jnp.max(matmul(tails, lm_head), axis=1).reshape(req_count, TAIL)
    peaks = peaks[:, TAIL - tail_count :]
    owners = jnp.arange(req_count, dtype=jnp.int32)
    found = (owners[:, None] ^ owners[None, :]) == lax.axis_index("req")
    peaks = jnp.sum(jnp.where(found[:, :, None], peaks[None], 0.0), axis=1).reshape(1, -1)
    for axis, bits in (("kv", kv_bits), ("req", req_bits)):
        for bit in bits:
            peaks = jnp.maximum(peaks, swap(peaks, axis, bit))
    return (layer_out, peaks[0])


def solution(mesh):
    placed = (
        P(("req", "kv"), None),
        P(),
        P("req"),
        P("req"),
        P("req", None, "kv"),
        P("req", None, "kv"),
        P("req", None, "kv"),
        P("req", None, "kv"),
        P(),
        P(None, "kv"),
        P(None, "kv"),
        P(None, "kv"),
        P(),
        P(),
        P("kv", None),
        P(),
        P(None, "req"),
        P(None, "req"),
        P("req", None),
        P(),
        P(None, ("req", "kv")),
    )
    return jax.shard_map(
        shards, mesh=mesh, in_specs=placed, out_specs=(P(("req", "kv"), None), P()), check_vma=False
    )
```

profile of v0, /device:TPU:0, one launch (start us, length us, event | category | flops | bytes accessed | tf_op | source)
XLA Modules:
  0.0 460.0 jit_solution(8972864708902901289)
XLA Ops:
  10.5 7.3 %all-to-all-start = ((bf16[32,8,2048]{2,1,0:T(8,128)(2,1)}), bf16[32,8,2048]{2,1,0:T(8,128)(2,1)S(1)}, u32[]{:S(2)}, u32[]{:S(2)}) async-start(bf16[32,8,2048]{2,1,0:T(8,128)(2,1)} %bitcast.3), calls=%async_computation | async-start | bytes 2097152 | tf_op jit(solution)/shard_map/all_to_all | solution.py:526
  25.0 19.0 %all-to-all-done = bf16[32,8,2048]{2,1,0:T(8,128)(2,1)S(1)} async-done(((bf16[32,8,2048]{2,1,0:T(8,128)(2,1)}), bf16[32,8,2048]{2,1,0:T(8,128)(2,1)S(1)}, u32[]{:S(2)}, u32[]{:S(2)}) %all-to-all-start) | async-done | bytes 1048608 | tf_op jit(solution)/shard_map/all_to_all | solution.py:526
  46.1 72.6 %shard_map.222 = bf16[768,1536]{1,0:T(8,128)(2,1)} custom-call(s32[1]{0:T(128)} %bitcast.5.index_ref, bf16[2048,768]{1,0:T(8,128)(2,1)} %refs_5_.1, bf16[2048,768]{1,0:T(8,128)(2,1)} %refs_6_.9, bf16[768,2048]{1,0:T(8,128)(2,1)} %refs_7_.9, bf16[256,2048]{1,0:T(8,128)(2,1)} %convolution_convert_fusion.3._), custom_call_target="tpu_custom_call" | custom-call | flops 1 | bytes 1 | tf_op jit(solution)/shard_map/pallas_call | solution.py:149
  121.5 6.1 %shard_map.213 = (bf16[256,512]{1,0:T(8,128)(2,1)}, bf16[256,256]{1,0:T(8,128)(2,1)}, bf16[256,256]{1,0:T(8,128)(2,1)}) custom-call(bf16[256,2048]{1,0:T(8,128)(2,1)} %collective-permute-done.refs_0_, f32[1,2048]{1,0:T(1,128)} %bitcast.37, f32[256,128]{1,0:T(8,128)} %get-tuple-element.82.refs_2_, f32[256,128]{1,0:T(8,128)} %get-tuple-element.78.refs_3_, ...), custom_call_target="tpu_custom_call" | custom-call | flops 1 | bytes 1 | tf_op jit(solution)/shard_map/pallas_call | solution.py:116
  129.2 6.1 %shard_map.212 = (bf16[256,512]{1,0:T(8,128)(2,1)}, bf16[256,256]{1,0:T(8,128)(2,1)}, bf16[256,256]{1,0:T(8,128)(2,1)}) custom-call(bf16[256,2048]{1,0:T(8,128)(2,1)} %copy-done.4, f32[1,2048]{1,0:T(1,128)} %bitcast.38, f32[256,128]{1,0:T(8,128)} %get-tuple-element.83.refs_2_, f32[256,128]{1,0:T(8,128)} %get-tuple-element.79.refs_3_, f32[1,128]{1,0:T(1,128)} %bitcast.44, ...), custom_call_target="tpu_custom_call" | custom-call | flops 1 | bytes 1 | tf_op jit(solution)/shard_map/pallas_call | solution.py:116
  135.4 6.1 %shard_map.215 = (bf16[256,512]{1,0:T(8,128)(2,1)}, bf16[256,256]{1,0:T(8,128)(2,1)}, bf16[256,256]{1,0:T(8,128)(2,1)}) custom-call(bf16[256,2048]{1,0:T(8,128)(2,1)} %shard_map.214.refs_0_, f32[1,2048]{1,0:T(1,128)} %bitcast.39, f32[256,128]{1,0:T(8,128)} %get-tuple-element.81.refs_2_, f32[256,128]{1,0:T(8,128)} %get-tuple-element.77.refs_3_, ...), custom_call_target="tpu_custom_call" | custom-call | flops 1 | bytes 1 | tf_op jit(solution)/shard_map/pallas_call | solution.py:116
  142.5 6.1 %shard_map.216 = (bf16[256,512]{1,0:T(8,128)(2,1)}, bf16[256,256]{1,0:T(8,128)(2,1)}, bf16[256,256]{1,0:T(8,128)(2,1)}) custom-call(bf16[256,2048]{1,0:T(8,128)(2,1)} %copy-done.18, f32[1,2048]{1,0:T(1,128)} %bitcast.40, f32[256,128]{1,0:T(8,128)} %get-tuple-element.80.refs_2_, f32[256,128]{1,0:T(8,128)} %get-tuple-element.76.refs_3_, f32[1,128]{1,0:T(1,128)} %bitcast.46, ...), custom_call_target="tpu_custom_call" | custom-call | flops 1 | bytes 1 | tf_op jit(solution)/shard_map/pallas_call | solution.py:116
  148.7 13.3 %shard_map.217 = (bf16[256,2048]{1,0:T(8,128)(2,1)}, bf16[256,2048]{1,0:T(8,128)(2,1)}, bf16[16,1536]{1,0:T(8,128)(2,1)}) custom-call(s32[10]{0:T(128)} %pad_add_fusion.lens_ref, bf16[256,512]{1,0:T(8,128)(2,1)} %get-tuple-element.48.refs_0_, bf16[256,512]{1,0:T(8,128)(2,1)} %get-tuple-element.49.refs_1_, bf16[256,256]{1,0:T(8,128)(2,1)} %get-tuple-element.40.refs_2_, ...), custom_call_target="tpu_custom_call" | custom-call | flops 1 | bytes 1 | tf_op jit(solution)/shard_map/pallas_call | solution.py:269
  162.6 11.9 %collective-permute-done.6 = bf16[768,1536]{1,0:T(8,128)(2,1)} collective-permute-done((bf16[768,1536]{1,0:T(8,128)(2,1)}, bf16[768,1536]{1,0:T(8,128)(2,1)}, u32[]{:S(2)}, u32[]{:S(2)}) %collective-permute-start.6) | collective-permute-done | bytes 2359328 | tf_op jit(solution)/shard_map/ppermute | solution.py:614
  177.0 10.8 %shard_map.218 = (f32[256,2048]{1,0:T(8,128)}, bf16[256,2048]{1,0:T(8,128)(2,1)}, bf16[16,1536]{1,0:T(8,128)(2,1)}) custom-call(s32[10]{0:T(128)} %pad_add_fusion.lens_ref, bf16[256,512]{1,0:T(8,128)(2,1)} %get-tuple-element.38.refs_0_, bf16[256,512]{1,0:T(8,128)(2,1)} %get-tuple-element.39.refs_1_, bf16[256,256]{1,0:T(8,128)(2,1)} %get-tuple-element.40.refs_2_, ...), custom_call_target="tpu_custom_call" | custom-call | flops 1 | bytes 1 | tf_op jit(solution)/shard_map/pallas_call | solution.py:269
  187.9 41.1 %collective-permute-done.7.refs_0_ = bf16[768,1536]{1,0:T(8,128)(2,1)S(1)} collective-permute-done((bf16[768,1536]{1,0:T(8,128)(2,1)}, bf16[768,1536]{1,0:T(8,128)(2,1)S(1)}, u32[]{:S(2)}, u32[]{:S(2)}) %collective-permute-start.7) | collective-permute-done | bytes 2359328 | tf_op jit(solution)/shard_map/ppermute | solution.py:614
  239.1 8.9 %shard_map.220.refs_4_ = bf16[16,2048]{1,0:T(8,128)(2,1)} custom-call(s32[10]{0:T(128)} %pad_add_fusion.lens_ref, bf16[16,1536]{1,0:T(8,128)(2,1)} %get-tuple-element.54.refs_0_, bf16[16,1536]{1,0:T(8,128)(2,1)} %get-tuple-element.55.refs_1_, bf16[512,2048]{1,0:T(8,128)(2,1)} %refs_2_.3, bf16[8,2048,256]{2,1,0:T(8,128)(2,1)} %refs_3_.3, ...), custom_call_target="tpu_custom_call" | custom-call | flops 1 | bytes 1 | tf_op jit(solution)/shard_map/pallas_call | solution.py:397
  250.0 12.9 %collective-permute-done.8.refs_0_ = bf16[256,2048]{1,0:T(8,128)(2,1)S(1)} collective-permute-done((bf16[256,2048]{1,0:T(8,128)(2,1)S(1)}, bf16[256,2048]{1,0:T(8,128)(2,1)S(1)}, u32[]{:S(2)}, u32[]{:S(2)}) %collective-permute-start.8) | collective-permute-done | bytes 1048608 | tf_op jit(solution)/shard_map/ppermute | solution.py:23
  270.4 8.5 %shard_map.221.refs_5_.refs_1_ = f32[256,2048]{1,0:T(8,128)} custom-call(bf16[256,2048]{1,0:T(8,128)(2,1)} %copy-done.3, bf16[2048,768]{1,0:T(8,128)(2,1)} %refs_5_.1, bf16[2048,768]{1,0:T(8,128)(2,1)} %refs_6_.9, bf16[768,2048]{1,0:T(8,128)(2,1)} %refs_7_.9, bf16[16,2048]{1,0:T(8,128)(2,1)} %shard_map.220.refs_4_), custom_call_target="tpu_custom_call" | custom-call | flops 1 | bytes 1 | tf_op jit(solution)/shard_map/pallas_call | solution.py:505
  279.0 21.1 %collective-permute-done.14.refs_8_.refs_3_ = bf16[16,2048]{1,0:T(8,128)(2,1)S(1)} collective-permute-done((bf16[16,2048]{1,0:T(8,128)(2,1)S(1)}, bf16[16,2048]{1,0:T(8,128)(2,1)S(1)}, u32[]{:S(2)}, u32[]{:S(2)}) %collective-permute-start.14) | collective-permute-done | bytes 65568 | tf_op jit(solution)/shard_map/ppermute | solution.py:23
  301.5 10.7 %shard_map.224 = (f32[256,2048]{1,0:T(8,128)}, f32[256,2048]{1,0:T(8,128)}) custom-call(bf16[256,2048]{1,0:T(8,128)(2,1)} %copy-done.16, bf16[256,2048]{1,0:T(8,128)(2,1)} %collective-permute-done.16.refs_1_, bf16[2048,768]{1,0:T(8,128)(2,1)} %refs_5_.1, bf16[2048,768]{1,0:T(8,128)(2,1)} %refs_6_.9, bf16[768,2048]{1,0:T(8,128)(2,1)} %refs_7_.9, ...), custom_call_target="tpu_custom_call" | custom-call | flops 1 | bytes 1 | tf_op jit(solution)/shard_map/pallas_call | solution.py:505
  313.2 8.9 %shard_map.225 = (f32[256,2048]{1,0:T(8,128)}, f32[16,2048]{1,0:T(8,128)}, f32[16,2048]{1,0:T(8,128)}, f32[16,2048]{1,0:T(8,128)}, f32[16,2048]{1,0:T(8,128)}) custom-call(bf16[256,2048]{1,0:T(8,128)(2,1)} %copy-done.12, bf16[16,2048]{1,0:T(8,128)(2,1)} %copy-done.19, bf16[16,2048]{1,0:T(8,128)(2,1)} %copy-done.21, bf16[16,2048]{1,0:T(8,128)(2,1)} %copy-done.22, ...), custom_call_target="tpu_custom_call" | custom-call | flops 1 | bytes 1 | tf_op jit(solution)/shard_map/pallas_call | solution.py:505
  322.1 11.4 %shard_map.226 = (bf16[256,2048]{1,0:T(8,128)(2,1)}, bf16[256,2048]{1,0:T(8,128)(2,1)}) custom-call(bf16[256,2048]{1,0:T(8,128)(2,1)} %copy-done.16, bf16[256,2048]{1,0:T(8,128)(2,1)} %collective-permute-done.16.refs_1_, f32[256,2048]{1,0:T(8,128)} %get-tuple-element.56.refs_8_.refs_2_, f32[256,2048]{1,0:T(8,128)} %get-tuple-element.62.refs_3_, ...), custom_call_target="tpu_custom_call" | custom-call | flops 1 | bytes 1 | tf_op jit(solution)/shard_map/pallas_call | solution.py:505
  333.5 5.1 %collective-permute-start.17 = (bf16[256,2048]{1,0:T(8,128)(2,1)}, bf16[256,2048]{1,0:T(8,128)(2,1)S(1)}, u32[]{:S(2)}, u32[]{:S(2)}) collective-permute-start(bf16[256,2048]{1,0:T(8,128)(2,1)} %get-tuple-element.63.refs_13_), channel_id=1, source_target_pairs={{0,4},{4,0},{8,12},{12,8},{16,20},{20,16},{24,28},{28,24},{1,5},{5... | collective-permute-start | bytes 3145736 | tf_op jit(solution)/shard_map/ppermute | solution.py:23
  338.8 9.1 %shard_map.227 = (bf16[256,2048]{1,0:T(8,128)(2,1)}, f32[16,2048]{1,0:T(8,128)}, bf16[16,2048]{1,0:T(8,128)(2,1)}, bf16[16,2048]{1,0:T(8,128)(2,1)}, bf16[16,2048]{1,0:T(8,128)(2,1)}) custom-call(bf16[256,2048]{1,0:T(8,128)(2,1)} %copy-done.12, bf16[16,2048]{1,0:T(8,128)(2,1)} %copy-done.19, bf16[16,2048]{1,0:T(8,128)(2,1)} %copy-done.21, ...), custom_call_target="tpu_custom_call" | custom-call | flops 1 | bytes 1 | tf_op jit(solution)/shard_map/pallas_call | solution.py:505
  351.5 32.9 %collective-permute-done.20 = bf16[16,2048]{1,0:T(8,128)(2,1)S(1)} collective-permute-done((bf16[16,2048]{1,0:T(8,128)(2,1)}, bf16[16,2048]{1,0:T(8,128)(2,1)S(1)}, u32[]{:S(2)}, u32[]{:S(2)}) %collective-permute-start.20) | collective-permute-done | bytes 65568 | tf_op jit(solution)/shard_map/ppermute | solution.py:23
  393.5 8.8 %shard_map.228.refs_1_ = f32[256,2048]{1,0:T(8,128)} custom-call(bf16[256,2048]{1,0:T(8,128)(2,1)} %copy-done.3, f32[256,2048]{1,0:T(8,128)} %shard_map.221.refs_5_.refs_1_, bf16[4,768,1536]{2,1,0:T(8,128)(2,1)} %bitcast.30, bf16[4,768,1536]{2,1,0:T(8,128)(2,1)} %bitcast.31, bf16[4,768,1536]{2,1,0:T(8,128)(2,1)} %bitcast.32, ...), custom_call_target="tpu_custom_call" | custom-call | flops 1 | bytes 1 | tf_op jit(solution)/shard_map/pallas_call | solution.py:505
  414.7 5.6 %all-to-all-start.1 = ((bf16[32,8,2048]{2,1,0:T(8,128)(2,1)}), bf16[32,8,2048]{2,1,0:T(8,128)(2,1)S(1)}, u32[]{:S(2)}, u32[]{:S(2)}) async-start(bf16[32,8,2048]{2,1,0:T(8,128)(2,1)} %fusion), calls=%async_computation.1 | async-start | bytes 2097152 | tf_op jit(solution)/shard_map/all_to_all | solution.py:526
  424.1 9.9 %convolution_reduce_fusion = f32[128]{0:T(128)S(1)} fusion(bf16[2048,4748]{0,1:T(8,128)(2,1)} %param.41, bf16[64,2048]{1,0:T(8,128)(2,1)S(1)} %collective-permute-done.25, bf16[64,2048]{1,0:T(8,128)(2,1)S(1)} %copy-done.17), kind=kOutput, calls=%fused_computation.14 | convolution fusion | flops 2490975744 | bytes 19972608 | tf_op jit(solution)/shard_map/dot_general | solution.py:530
  (167 shorter events, 87.3 us)
Async XLA Ops:
  10.5 33.5 %all-to-all-start = ((bf16[32,8,2048]{2,1,0:T(8,128)(2,1)}), bf16[32,8,2048]{2,1,0:T(8,128)(2,1)S(1)}, u32[]{:S(2)}, u32[]{:S(2)}) async-start(bf16[32,8,2048]{2,1,0:T(8,128)(2,1)} %bitcast.3), calls=%async_computation | async-start | bytes 2097152 | tf_op jit(solution)/shard_map/all_to_all | solution.py:526
  17.8 304.3 %all-gather.3.cloned.1.call-start = ((), (), s32[]{:S(2)}) async-start(), calls=%async_computation.2 | async-start | bytes 11796480 | tf_op jit(solution)/shard_map/all_gather | solution.py:656
  44.5 77.0 %collective-permute-start = (bf16[256,2048]{1,0:T(8,128)(2,1)S(1)}, bf16[256,2048]{1,0:T(8,128)(2,1)}, u32[]{:S(2)}, u32[]{:S(2)}) collective-permute-start(bf16[256,2048]{1,0:T(8,128)(2,1)S(1)} %convolution_convert_fusion.2.refs_0_), channel_id=1, source_target_pairs={{0,1},{1,0},{2,3},{3,2},{4,5},{5,4},{6,7},{7,6},{8,9},{9,8},{10,11... | collective-permute-start | bytes 3145736 | tf_op jit(solution)/shard_map/ppermute | solution.py:23
  44.6 83.1 %collective-permute-start.1 = (bf16[256,2048]{1,0:T(8,128)(2,1)S(1)}, bf16[256,2048]{1,0:T(8,128)(2,1)S(1)}, u32[]{:S(2)}, u32[]{:S(2)}) collective-permute-start(bf16[256,2048]{1,0:T(8,128)(2,1)S(1)} %convolution_convert_fusion.2.refs_0_), channel_id=1, source_target_pairs={{0,2},{1,3},{2,0},{3,1},{4,6},{5,7},{6,4},{7,5},{8,10},{9,11},{10,... | collective-permute-start | bytes 3145736 | tf_op jit(solution)/shard_map/ppermute | solution.py:23
  118.7 55.7 %collective-permute-start.6 = (bf16[768,1536]{1,0:T(8,128)(2,1)}, bf16[768,1536]{1,0:T(8,128)(2,1)}, u32[]{:S(2)}, u32[]{:S(2)}) collective-permute-start(bf16[768,1536]{1,0:T(8,128)(2,1)} %shard_map.222), channel_id=1, source_target_pairs={{0,8},{4,12},{8,16},{12,20},{16,24},{20,28},{24,0},{28,4},{1,9},{5... | collective-permute-start | bytes 7077896 | tf_op jit(solution)/shard_map/ppermute | solution.py:614
  128.6 12.9 %collective-permute-start.2 = (bf16[256,2048]{1,0:T(8,128)(2,1)}, bf16[256,2048]{1,0:T(8,128)(2,1)S(1)}, u32[]{:S(2)}, u32[]{:S(2)}) collective-permute-start(bf16[256,2048]{1,0:T(8,128)(2,1)} %shard_map.214.refs_0_), channel_id=1, source_target_pairs={{0,1},{1,0},{2,3},{3,2},{4,5},{5,4},{6,7},{7,6},{8,9},{9,8},{10,11... | collective-permute-start | bytes 3145736 | tf_op jit(solution)/shard_map/ppermute | solution.py:23
  162.0 12.5 %collective-permute-start.3 = (bf16[256,2048]{1,0:T(8,128)(2,1)}, bf16[256,2048]{1,0:T(8,128)(2,1)S(1)}, u32[]{:S(2)}, u32[]{:S(2)}) collective-permute-start(bf16[256,2048]{1,0:T(8,128)(2,1)} %get-tuple-element.51), channel_id=1, source_target_pairs={{0,1},{1,0},{2,3},{3,2},{4,5},{5,4},{6,7},{7,6},{8,9},{9,8},{10,11... | collective-permute-start | bytes 3145736 | tf_op jit(solution)/shard_map/ppermute | solution.py:23
  174.4 54.5 %collective-permute-start.7 = (bf16[768,1536]{1,0:T(8,128)(2,1)}, bf16[768,1536]{1,0:T(8,128)(2,1)S(1)}, u32[]{:S(2)}, u32[]{:S(2)}) collective-permute-start(bf16[768,1536]{1,0:T(8,128)(2,1)} %collective-permute-done.6), channel_id=1, source_target_pairs={{0,8},{4,12},{8,16},{12,20},{16,24},{20,28},{24,0},{28,4},{1,9},{5... | collective-permute-start | bytes 7077896 | tf_op jit(solution)/shard_map/ppermute | solution.py:614
  176.1 52.9 %collective-permute-start.4 = (bf16[256,2048]{1,0:T(8,128)(2,1)S(1)}, bf16[256,2048]{1,0:T(8,128)(2,1)S(1)}, u32[]{:S(2)}, u32[]{:S(2)}) collective-permute-start(bf16[256,2048]{1,0:T(8,128)(2,1)S(1)} %add_convert_fusion.1.refs_13_), channel_id=1, source_target_pairs={{0,2},{1,3},{2,0},{3,1},{4,6},{5,7},{6,4},{7,5},{8,10},{9,11},{10,... | collective-permute-start | bytes 3145736 | tf_op jit(solution)/shard_map/ppermute | solution.py:23
  237.6 25.3 %collective-permute-start.8 = (bf16[256,2048]{1,0:T(8,128)(2,1)S(1)}, bf16[256,2048]{1,0:T(8,128)(2,1)S(1)}, u32[]{:S(2)}, u32[]{:S(2)}) collective-permute-start(bf16[256,2048]{1,0:T(8,128)(2,1)S(1)} %fusion.3.refs_5_.refs_0_), channel_id=1, source_target_pairs={{0,4},{4,0},{8,12},{12,8},{16,20},{20,16},{24,28},{28,24},{1,5},{5... | collective-permute-start | bytes 3145736 | tf_op jit(solution)/shard_map/ppermute | solution.py:23
  248.0 14.8 %collective-permute-start.10 = (bf16[16,2048]{1,0:T(8,128)(2,1)}, bf16[16,2048]{1,0:T(8,128)(2,1)S(1)}, u32[]{:S(2)}, u32[]{:S(2)}) collective-permute-start(bf16[16,2048]{1,0:T(8,128)(2,1)} %shard_map.220.refs_4_), channel_id=1, source_target_pairs={{0,1},{1,0},{2,3},{3,2},{4,5},{5,4},{6,7},{7,6},{8,9},{9,8},{10,11... | collective-permute-start | bytes 196616 | tf_op jit(solution)/shard_map/ppermute | solution.py:23
  248.1 14.7 %collective-permute-start.11 = (bf16[16,2048]{1,0:T(8,128)(2,1)}, bf16[16,2048]{1,0:T(8,128)(2,1)S(1)}, u32[]{:S(2)}, u32[]{:S(2)}) collective-permute-start(bf16[16,2048]{1,0:T(8,128)(2,1)} %shard_map.220.refs_4_), channel_id=1, source_target_pairs={{0,2},{1,3},{2,0},{3,1},{4,6},{5,7},{6,4},{7,5},{8,10},{9,11},{10,... | collective-permute-start | bytes 196616 | tf_op jit(solution)/shard_map/ppermute | solution.py:23
  248.7 14.1 %collective-permute-start.12 = (bf16[16,2048]{1,0:T(8,128)(2,1)}, bf16[16,2048]{1,0:T(8,128)(2,1)S(1)}, u32[]{:S(2)}, u32[]{:S(2)}) collective-permute-start(bf16[16,2048]{1,0:T(8,128)(2,1)} %shard_map.220.refs_4_), channel_id=1, source_target_pairs={{0,3},{1,2},{2,1},{3,0},{4,7},{5,6},{6,5},{7,4},{8,11},{9,10},{10,... | collective-permute-start | bytes 196616 | tf_op jit(solution)/shard_map/ppermute | solution.py:23
  250.0 50.9 %collective-permute-start.16 = (bf16[256,2048]{1,0:T(8,128)(2,1)}, bf16[256,2048]{1,0:T(8,128)(2,1)}, u32[]{:S(2)}, u32[]{:S(2)}) collective-permute-start(bf16[256,2048]{1,0:T(8,128)(2,1)} %copy-done.3), channel_id=1, source_target_pairs={{0,8},{4,12},{8,0},{12,4},{16,24},{20,28},{24,16},{28,20},{1,9},{5... | collective-permute-start | bytes 3145736 | tf_op jit(solution)/shard_map/ppermute | solution.py:23
  262.8 49.4 %collective-permute-start.9 = (bf16[256,2048]{1,0:T(8,128)(2,1)S(1)}, bf16[256,2048]{1,0:T(8,128)(2,1)S(1)}, u32[]{:S(2)}, u32[]{:S(2)}) collective-permute-start(bf16[256,2048]{1,0:T(8,128)(2,1)S(1)} %collective-permute-done.8.refs_0_), channel_id=1, source_target_pairs={{0,8},{4,12},{8,0},{12,4},{16,24},{20,28},{24,16},{28,20},{1,9},{5... | collective-permute-start | bytes 3145736 | tf_op jit(solution)/shard_map/ppermute | solution.py:23
  266.0 34.1 %collective-permute-start.14 = (bf16[16,2048]{1,0:T(8,128)(2,1)S(1)}, bf16[16,2048]{1,0:T(8,128)(2,1)S(1)}, u32[]{:S(2)}, u32[]{:S(2)}) collective-permute-start(bf16[16,2048]{1,0:T(8,128)(2,1)S(1)} %fusion.18.refs_6_.refs_1_), channel_id=1, source_target_pairs={{0,8},{4,12},{8,0},{12,4},{16,24},{20,28},{24,16},{28,20},{1,9},{5... | collective-permute-start | bytes 196616 | tf_op jit(solution)/shard_map/ppermute | solution.py:23
  268.7 32.1 %collective-permute-start.15 = (bf16[16,2048]{1,0:T(8,128)(2,1)S(1)}, bf16[16,2048]{1,0:T(8,128)(2,1)S(1)}, u32[]{:S(2)}, u32[]{:S(2)}) collective-permute-start(bf16[16,2048]{1,0:T(8,128)(2,1)S(1)} %collective-permute-done.13.refs_7_.refs_2_), channel_id=1, source_target_pairs={{0,8},{4,12},{8,0},{12,4},{16,24},{20,28},{24,16},{28,20},{1,9},{5... | collective-permute-start | bytes 196616 | tf_op jit(solution)/shard_map/ppermute | solution.py:23
  333.5 58.1 %collective-permute-start.17 = (bf16[256,2048]{1,0:T(8,128)(2,1)}, bf16[256,2048]{1,0:T(8,128)(2,1)S(1)}, u32[]{:S(2)}, u32[]{:S(2)}) collective-permute-start(bf16[256,2048]{1,0:T(8,128)(2,1)} %get-tuple-element.63.refs_13_), channel_id=1, source_target_pairs={{0,4},{4,0},{8,12},{12,8},{16,20},{20,16},{24,28},{28,24},{1,5},{5... | collective-permute-start | bytes 3145736 | tf_op jit(solution)/shard_map/ppermute | solution.py:23
  338.5 53.1 %collective-permute-start.18 = (bf16[256,2048]{1,0:T(8,128)(2,1)}, bf16[256,2048]{1,0:T(8,128)(2,1)S(1)}, u32[]{:S(2)}, u32[]{:S(2)}) collective-permute-start(bf16[256,2048]{1,0:T(8,128)(2,1)} %get-tuple-element.65), channel_id=1, source_target_pairs={{0,8},{4,12},{8,0},{12,4},{16,24},{20,28},{24,16},{28,20},{1,9},{5... | collective-permute-start | bytes 3145736 | tf_op jit(solution)/shard_map/ppermute | solution.py:23
  347.9 55.8 %collective-permute-start.19 = (bf16[256,2048]{1,0:T(8,128)(2,1)}, bf16[256,2048]{1,0:T(8,128)(2,1)}, u32[]{:S(2)}, u32[]{:S(2)}) collective-permute-start(bf16[256,2048]{1,0:T(8,128)(2,1)} %get-tuple-element.64.refs_5_), channel_id=1, source_target_pairs={{0,12},{4,8},{8,4},{12,0},{16,28},{20,24},{24,20},{28,16},{1,13},{... | collective-permute-start | bytes 3145736 | tf_op jit(solution)/shard_map/ppermute | solution.py:23
  349.2 35.3 %collective-permute-start.20 = (bf16[16,2048]{1,0:T(8,128)(2,1)}, bf16[16,2048]{1,0:T(8,128)(2,1)S(1)}, u32[]{:S(2)}, u32[]{:S(2)}) collective-permute-start(bf16[16,2048]{1,0:T(8,128)(2,1)} %get-tuple-element.67), channel_id=1, source_target_pairs={{0,4},{4,0},{8,12},{12,8},{16,20},{20,16},{24,28},{28,24},{1,5},{5... | collective-permute-start | bytes 196616 | tf_op jit(solution)/shard_map/ppermute | solution.py:23
  351.2 36.6 %collective-permute-start.21 = (bf16[16,2048]{1,0:T(8,128)(2,1)}, bf16[16,2048]{1,0:T(8,128)(2,1)S(1)}, u32[]{:S(2)}, u32[]{:S(2)}) collective-permute-start(bf16[16,2048]{1,0:T(8,128)(2,1)} %get-tuple-element.68), channel_id=1, source_target_pairs={{0,8},{4,12},{8,0},{12,4},{16,24},{20,28},{24,16},{28,20},{1,9},{5... | collective-permute-start | bytes 196616 | tf_op jit(solution)/shard_map/ppermute | solution.py:23
  413.2 11.0 %collective-permute-start.25 = (bf16[64,2048]{1,0:T(8,128)(2,1)}, bf16[64,2048]{1,0:T(8,128)(2,1)S(1)}, u32[]{:S(2)}, u32[]{:S(2)}) collective-permute-start(bf16[64,2048]{1,0:T(8,128)(2,1)} %shard_map.230), channel_id=1, source_target_pairs={{0,16},{4,20},{8,24},{12,28},{16,0},{20,4},{24,8},{28,12},{1,17},{... | collective-permute-start | bytes 786440 | tf_op jit(solution)/shard_map/ppermute | solution.py:23
  414.7 36.5 %all-to-all-start.1 = ((bf16[32,8,2048]{2,1,0:T(8,128)(2,1)}), bf16[32,8,2048]{2,1,0:T(8,128)(2,1)S(1)}, u32[]{:S(2)}, u32[]{:S(2)}) async-start(bf16[32,8,2048]{2,1,0:T(8,128)(2,1)} %fusion), calls=%async_computation.1 | async-start | bytes 2097152 | tf_op jit(solution)/shard_map/all_to_all | solution.py:526
  (37 other events, 294.6 us)
Sparse Core Ops, SparseCore 0:
  230.8 64.2 all-gather.2
where the time goes:
time: 465 us; the launch traced here: 460 us
  Pallas kernels  188 us (40%)
  waiting for transfers between devices  168 us (36%)
  starting transfers between devices  40.8 us (9%)
  between operations  18.4 us (4%)
  other arithmetic  16.7 us (4%)
  matrix products  15.1 us (3%)
  local copies, waits for them, and re-layouts  13.4 us (3%)
    ppermute x29, waiting for transfers between devices, swap(): return lax.ppermute(value, axis, [(i, i ^ bit) for i in range(size)])  96.1 us
    pallas_call x1, Pallas kernels, share_of(): pl.pallas_call(functools.partial(share_kernel, share, tile), out_shape=ja...  72.6 us
    pallas_call x6, Pallas kernels, feed_forward(): pl.pallas_call(kernel, out_shape=[jax.ShapeDtypeStruct((count, width), dt...  57.4 us
    ppermute x2, waiting for transfers between devices, shards(): far_shares.append(lax.ppermute(far_shares[-1], 'req', ring))  52.9 us
    ppermute x29, starting transfers between devices, swap(): return lax.ppermute(value, axis, [(i, i ^ bit) for i in range(size)])  26.7 us
    pallas_call x4, Pallas kernels, project(): pl.pallas_call(functools.partial(project_kernel, len(blocks), head_dim),...  24.5 us
    pallas_call x2, Pallas kernels, attend(): pl.pallas_call(functools.partial(attend_kernel, pair, block_count, head_d...  24.2 us
    all_to_all x2, waiting for transfers between devices, regroup(): lax.all_to_all(rows_in, ('req', 'kv'), split_axis=0, concat_axis=0, tiled...  19 us
  transfers between devices with their start and end apart: 34, of which 19 were waited for; matrix products, arithmetic and copies ran while one was open for 6% of the time, Pallas kernels for 38%

commit v1 on v0

--- a/solution.py
+++ b/solution.py
@@ -107,7 +107,7 @@
     v_ref[...] = matmul(rows, wv[...]).astype(jnp.bfloat16)
 
 
-def project(blocks, gain, cosine, sine, q_gain, k_gain, q_proj, k_proj, v_proj):
+def project(blocks, gain, cosine, sine, q_gain, k_gain, q_proj, k_proj, v_proj, follows):
     head_dim = q_gain.shape[0]
     rows = sum(block.shape[0] for block in blocks)
     width = q_proj.shape[0]
@@ -118,14 +118,14 @@
         out_shape=[jax.ShapeDtypeStruct((rows, cols), jnp.bfloat16) for cols in outs],
         in_specs=[whole_spec(block.shape) for block in blocks]
         + [whole_spec(vector.shape) for vector in vectors]
-        + [pl.BlockSpec(memory_space=pl.ANY)] * 3,
+        + [pl.BlockSpec(memory_space=pl.ANY)] * 4,
         out_specs=[whole_spec((rows, cols)) for cols in outs],
         grid=(1,),
         scratch_shapes=[pltpu.VMEM((width, cols), jnp.bfloat16) for cols in outs]
         + [pltpu.SemaphoreType.DMA((3,))],
         compiler_params=pltpu.CompilerParams(vmem_limit_bytes=VMEM_LIMIT),
         cost_estimate=BRIEF,
-    )(*blocks, *vectors, q_proj, k_proj, v_proj)
+    )(*blocks, *vectors, q_proj, k_proj, v_proj, follows)
 
 
 def share_kernel(share, tile, index_ref, gate, up, down, _, out, sems):
@@ -150,7 +150,7 @@
         functools.partial(share_kernel, share, tile),
         out_shape=jax.ShapeDtypeStruct((share + tile, 2 * hidden), gate.dtype),
         in_specs=[pl.BlockSpec(memory_space=pltpu.SMEM)] + [pl.BlockSpec(memory_space=pl.ANY)] * 4,
-        out_specs=pl.BlockSpec(memory_space=pl.ANY),
+        out_specs=pl.BlockSpec(memory_space=pltpu.VMEM),
         scratch_shapes=[pltpu.SemaphoreType.DMA((2 + hidden // tile,))],
         cost_estimate=BRIEF,
     )(index, gate, up, down, follows)
@@ -161,7 +161,7 @@
     k_refs, refs = refs[:block_count], refs[block_count:]
     v_refs, refs = refs[:block_count], refs[block_count:]
     sources, refs = refs[:3], refs[3 + 1 :]
-    even_ref, odd_ref, last_ref, k_all, v_all, peak, acc, attended, kp, vp, weight, sems = refs
+    even_ref, *odd_refs, last_ref, k_all, v_all, peak, acc, attended, kp, vp, weight, sems = refs
     copies = [
         pltpu.make_async_copy(source, target, sems.at[at])
         for at, (source, target) in enumerate(zip(sources, (kp, vp, weight)))
@@ -242,7 +242,9 @@
     for at in range(0, width, q_cols):
         part = matmul(attended[...], weight[:, at : at + q_cols])
         even_ref[:, at : at + q_cols] = part[:rows].astype(even_ref.dtype)
-        odd_ref[:, at : at + q_cols] = part[rows:].astype(odd_ref.dtype)
+        for half, odd_ref in enumerate(odd_refs):
+            here = rows + half * (rows // 2)
+            odd_ref[:, at : at + q_cols] = part[here : here + rows // 2].astype(odd_ref.dtype)
     last = kv_index ^ (block_count - 1)
     here = pl.multiple_of((last % 2) * rows + rows - TAIL, TAIL)
     last_ref[:, :q_cols] = attended[pl.ds(here, TAIL), :]
@@ -263,7 +265,8 @@
     heads = q_cols // head_dim
     outs = [
         jax.ShapeDtypeStruct((rows, width), even_type),
-        jax.ShapeDtypeStruct((rows, width), jnp.bfloat16),
+        jax.ShapeDtypeStruct((rows // 2, width), jnp.bfloat16),
+        jax.ShapeDtypeStruct((rows // 2, width), jnp.bfloat16),
         jax.ShapeDtypeStruct((TAIL, 2 * q_cols + 2 * kv_cols), jnp.bfloat16),
     ]
     return pl.pallas_call(
@@ -609,32 +612,35 @@
     far_share = share_of(kv_index[None], width // kv_count, w_gate, w_up, w_down, sent)
     step = GROUP if far_count > 2 else GROUP // 2
     ring = [(i, (i + step) % req_count) for i in range(req_count)]
-    far_shares = [far_share]
+    far_hops = [far_share]
     for _ in range(max(2, far_count - 1)):
-        far_shares.append(lax.ppermute(far_shares[-1], "req", ring))
-    far_shares = far_shares[GROUP // step :]
+        far_hops.append(lax.ppermute(far_hops[-1], "req", ring))
+    far_shares = far_hops[GROUP // step :]
     arrived = regroup(sent)
     owner_rows = pick(slot_hot, arrived)
 
-    def project_block(diff):
+    def project_block(diff, follows):
         block_at = (kv_index ^ diff) * rows_dev
         tables = [lax.dynamic_slice_in_dim(table, block_at, rows_dev, 0) for table in (cosines, sines)]
-        return project([blocks[diff]], attn_gain, *tables, q_gain, k_gain, q_proj, k_proj, v_proj)
+        return project(
+            [blocks[diff]], attn_gain, *tables, q_gain, k_gain, q_proj, k_proj, v_proj, follows
+        )
 
     even = gather_xor(owner_rows, "kv", kv_bits[:0:-1])
     blocks = {0: owner_rows, 1: swap(owner_rows, "kv", 1)}
-    parts = [project_block(0), project_block(1)]
+    parts = [project_block(0, owner_rows)]
+    parts.append(project_block(1, parts[0][2]))
     for diff in range(2, kv_count, 2):
         blocks[diff] = pin(even[diff], parts[1][2])
         blocks[diff + 1] = swap(blocks[diff], "kv", 1)
     for diff in range(2, kv_count):
-        parts.append(project_block(diff))
+        parts.append(project_block(diff, far_hops[1] if diff == 2 else parts[-1][2]))
 
     f32, bf16 = jnp.float32, jnp.bfloat16
     lens = jnp.concatenate([kv_index[None], prefill_start, cache_len]).astype(jnp.int32)
     follows, lasts, sums = parts[-1][2], {}, []
     for pair in range(kv_count // 2 - 1, -1, -1):
-        sum_even, sum_odd, lasts[pair] = attend(
+        sum_even, *sum_odd, lasts[pair] = attend(
             pair,
             lens,
             parts,
@@ -646,14 +652,16 @@
             follows,
         )
         if pair:
-            both = sum_even.astype(f32) + swap(sum_odd, "kv", 1).astype(f32)
+            other = jnp.concatenate([swap(half, "kv", 1) for half in sum_odd], axis=0)
+            both = sum_even.astype(f32) + other.astype(f32)
             follows = both.astype(bf16)
             sums.append(swap(follows, "kv", 2 * pair))
         else:
-            sums.append(swap(pin(sum_odd, *sums), "kv", 1))
+            halves = [swap(pin(half, *sums, *far_shares), "kv", 1) for half in sum_odd]
+            sums.append(jnp.concatenate(halves, axis=0))
             own_sum = sum_even
     far_weights = [
-        lax.all_gather(pin(held, own_sum, *sums[:-1]), "kv") for held in far_shares
+        lax.all_gather(pin(held, own_sum), "kv") for held in far_shares
     ]
     resid = owner_rows.astype(f32) + own_sum
     for each in sums:
@@ -689,14 +697,15 @@
 
     zero = feed_forward([ffn_in], [f32], [own_weights], [last_sum])
     near[3] = swap(near[1], "req", 2)
-    some = feed_forward([near[1], near[2]], [f32] * 2, [own_weights], [zero[0], *lasts_in])
+    some = feed_forward([near[1], near[2]], [f32] * 2, [own_weights], [zero[0], last_near[1]])
     rest = feed_forward([near[3], *lasts_in], [f32] * (1 + GROUP), [own_weights], some[:1])
     first, second = feed_forward([near[1], near[2]], [bf16] * 2, far_weights, rest[:1], some)
     third, last_part, *last_parts = feed_forward(
         [near[3], *lasts_in], [bf16, f32] + [bf16] * (GROUP - 1), far_weights, [first], rest
     )
     backs = [swap(first, "req", 1), swap(second, "req", 2), swap(third, "req", 3)]
-    (own_part,) = feed_forward([ffn_in], [f32], far_weights, [third, *backs[:2]], zero)
+    (own_part,) = feed_forward([ffn_in], [f32], far_weights, [third, backs[0][:TAIL], backs[1][:TAIL]], zero)
+    last_part = pin(last_part, own_part)
     for diff, part in enumerate(last_parts, 1):
         last_part = last_part + swap(part, "req", diff).astype(f32)
     last_rows = (last_resid.astype(f32) + last_part).astype(bf16)
@@ -710,12 +719,11 @@
     layer_out = pick(send_hot, returned, transposed=True)
 
     tail_count = dec_count + 1
-    tails = pin(norm_rows(last_rows, final_gain).astype(bf16), own_part)
+    tails = norm_rows(last_rows, final_gain).astype(bf16)
     req_bits = bits_below(req_count)
     for bit in req_bits:
-        if bit == req_bits[-1]:
-            tails = pin(tails, out_rows)
         tails = jnp.concatenate([tails, swap(tails, "req", bit)], axis=0)
+    tails = pin(tails, out_rows)
     peaks = jnp.max(matmul(tails, lm_head), axis=1).reshape(req_count, TAIL)
     peaks = peaks[:, TAIL - tail_count :]
     owners = jnp.arange(req_count, dtype=jnp.int32)

time: 465 us -> 409 us (0.88)
  Pallas kernels: 188 us -> 133 us
  waiting for transfers between devices: 168 us -> 156 us
  starting transfers between devices: 40.8 us -> 51 us
    pallas_call x1, Pallas kernels: 72.6 us -> 3.1 us  [share_of(): pl.pallas_call(functools.partial(share_kernel, share, tile), out_shape=ja...]
    ppermute x2, waiting for transfers between devices: 52.9 us -> 0.01 us  [shards(): far_hops.append(lax.ppermute(far_hops[-1], 'req', ring))]
    all_to_all x2, waiting for transfers between devices: 19 us -> 65.3 us  [regroup(): lax.all_to_all(rows_in, ('req', 'kv'), split_axis=0, concat_axis=0, tiled...]
    pallas_call x2, Pallas kernels: 24.2 us -> 39.6 us  [attend(): pl.pallas_call(functools.partial(attend_kernel, pair, block_count, head_d...]
    ppermute x29 -> x31, starting transfers between devices: 26.7 us -> 37.8 us  [swap(): return lax.ppermute(value, axis, [(i, i ^ bit) for i in range(size)])]
    ppermute x29 -> x31, waiting for transfers between devices: 96.1 us -> 89.6 us  [swap(): return lax.ppermute(value, axis, [(i, i ^ bit) for i in range(size)])]
  transfers between devices with their start and end apart: 34 -> 36, of which waited for: 19 -> 20; matrix products, arithmetic and copies ran while one was open for 6% -> 8% of each run, Pallas kernels for 38% -> 30%
where the time goes in v1:
time: 409 us; the launch traced here: 402 us
  waiting for transfers between devices  156 us (38%)
  Pallas kernels  133 us (33%)
  starting transfers between devices  51 us (12%)
  between operations  17.7 us (4%)
  other arithmetic  16.2 us (4%)
  matrix products  14.8 us (4%)
  local copies, waits for them, and re-layouts  13.5 us (3%)
    ppermute x31, waiting for transfers between devices, swap(): return lax.ppermute(value, axis, [(i, i ^ bit) for i in range(size)])  89.6 us
    all_to_all x2, waiting for transfers between devices, regroup(): lax.all_to_all(rows_in, ('req', 'kv'), split_axis=0, concat_axis=0, tiled...  65.3 us
    pallas_call x6, Pallas kernels, feed_forward(): pl.pallas_call(kernel, out_shape=[jax.ShapeDtypeStruct((count, width), dt...  57.9 us
    pallas_call x2, Pallas kernels, attend(): pl.pallas_call(functools.partial(attend_kernel, pair, block_count, head_d...  39.6 us
    ppermute x31, starting transfers between devices, swap(): return lax.ppermute(value, axis, [(i, i ^ bit) for i in range(size)])  37.8 us
    pallas_call x4, Pallas kernels, project(): pl.pallas_call(functools.partial(project_kernel, len(blocks), head_dim),...  24.5 us
    dot_general x4, matrix products, matmul(): return jnp.dot(left, right, preferred_element_type=jnp.float32)  11.7 us
    all_to_all x2, starting transfers between devices, regroup(): lax.all_to_all(rows_in, ('req', 'kv'), split_axis=0, concat_axis=0, tiled...  10.1 us
  transfers between devices with their start and end apart: 36, of which 20 were waited for; matrix products, arithmetic and copies ran while one was open for 8% of the time, Pallas kernels for 30%

profile of v1, /device:TPU:0, one launch (start us, length us, event | category | flops | bytes accessed | tf_op | source)
XLA Modules:
  0.0 401.8 jit_solution(18328449726702476751)
XLA Ops:
  10.4 7.3 %all-to-all-start = ((bf16[32,8,2048]{2,1,0:T(8,128)(2,1)}), bf16[32,8,2048]{2,1,0:T(8,128)(2,1)S(1)}, u32[]{:S(2)}, u32[]{:S(2)}) async-start(bf16[32,8,2048]{2,1,0:T(8,128)(2,1)} %bitcast.3), calls=%async_computation | async-start | bytes 2097152 | tf_op jit(solution)/shard_map/all_to_all | solution.py:529
  29.2 65.3 %all-to-all-done = bf16[32,8,2048]{2,1,0:T(8,128)(2,1)S(1)} async-done(((bf16[32,8,2048]{2,1,0:T(8,128)(2,1)}), bf16[32,8,2048]{2,1,0:T(8,128)(2,1)S(1)}, u32[]{:S(2)}, u32[]{:S(2)}) %all-to-all-start) | async-done | bytes 1048608 | tf_op jit(solution)/shard_map/all_to_all | solution.py:529
  98.3 6.1 %shard_map.212 = (bf16[256,512]{1,0:T(8,128)(2,1)}, bf16[256,256]{1,0:T(8,128)(2,1)}, bf16[256,256]{1,0:T(8,128)(2,1)}) custom-call(bf16[256,2048]{1,0:T(8,128)(2,1)} %copy-done.4, f32[1,2048]{1,0:T(1,128)} %bitcast.38, f32[256,128]{1,0:T(8,128)} %get-tuple-element.87.refs_2_, f32[256,128]{1,0:T(8,128)} %get-tuple-element.83.refs_3_, f32[1,128]{1,0:T(1,128)} %bitcast.44, ...), custom_call_target="tpu_custom_call" | custom-call | flops 1 | bytes 1 | tf_op jit(solution)/shard_map/pallas_call | solution.py:116
  104.4 6.1 %shard_map.213 = (bf16[256,512]{1,0:T(8,128)(2,1)}, bf16[256,256]{1,0:T(8,128)(2,1)}, bf16[256,256]{1,0:T(8,128)(2,1)}) custom-call(bf16[256,2048]{1,0:T(8,128)(2,1)} %collective-permute-done.refs_0_, f32[1,2048]{1,0:T(1,128)} %bitcast.39, f32[256,128]{1,0:T(8,128)} %get-tuple-element.86.refs_2_, f32[256,128]{1,0:T(8,128)} %get-tuple-element.82.refs_3_, ...), custom_call_target="tpu_custom_call" | custom-call | flops 1 | bytes 1 | tf_op jit(solution)/shard_map/pallas_call | solution.py:116
  110.6 10.1 %collective-permute-done.1.refs_0_ = bf16[256,2048]{1,0:T(8,128)(2,1)S(1)} collective-permute-done((bf16[256,2048]{1,0:T(8,128)(2,1)S(1)}, bf16[256,2048]{1,0:T(8,128)(2,1)S(1)}, u32[]{:S(2)}, u32[]{:S(2)}) %collective-permute-start.1) | collective-permute-done | bytes 1048608 | tf_op jit(solution)/shard_map/ppermute | solution.py:23
  123.6 6.1 %shard_map.216 = (bf16[256,512]{1,0:T(8,128)(2,1)}, bf16[256,256]{1,0:T(8,128)(2,1)}, bf16[256,256]{1,0:T(8,128)(2,1)}) custom-call(bf16[256,2048]{1,0:T(8,128)(2,1)} %shard_map.214.refs_0_, f32[1,2048]{1,0:T(1,128)} %bitcast.40, f32[256,128]{1,0:T(8,128)} %get-tuple-element.85.refs_2_, f32[256,128]{1,0:T(8,128)} %get-tuple-element.81.refs_3_, ...), custom_call_target="tpu_custom_call" | custom-call | flops 1 | bytes 1 | tf_op jit(solution)/shard_map/pallas_call | solution.py:116
  130.7 6.1 %shard_map.217 = (bf16[256,512]{1,0:T(8,128)(2,1)}, bf16[256,256]{1,0:T(8,128)(2,1)}, bf16[256,256]{1,0:T(8,128)(2,1)}) custom-call(bf16[256,2048]{1,0:T(8,128)(2,1)} %copy-done.17, f32[1,2048]{1,0:T(1,128)} %bitcast.41, f32[256,128]{1,0:T(8,128)} %get-tuple-element.84.refs_2_, f32[256,128]{1,0:T(8,128)} %get-tuple-element.80.refs_3_, f32[1,128]{1,0:T(1,128)} %bitcast.47, ...), custom_call_target="tpu_custom_call" | custom-call | flops 1 | bytes 1 | tf_op jit(solution)/shard_map/pallas_call | solution.py:116
  136.9 20.9 %shard_map.218 = (bf16[256,2048]{1,0:T(8,128)(2,1)}, bf16[128,2048]{1,0:T(8,128)(2,1)}, bf16[128,2048]{1,0:T(8,128)(2,1)}, bf16[16,1536]{1,0:T(8,128)(2,1)}) custom-call(s32[10]{0:T(128)} %pad_add_fusion.lens_ref, bf16[256,512]{1,0:T(8,128)(2,1)} %get-tuple-element.50.refs_0_, bf16[256,512]{1,0:T(8,128)(2,1)} %get-tuple-element.51.refs_1_, ...), custom_call_target="tpu_custom_call" | custom-call | flops 1 | bytes 1 | tf_op jit(solution)/shard_map/pallas_call | solution.py:272
  163.4 18.7 %shard_map.219 = (f32[256,2048]{1,0:T(8,128)}, bf16[128,2048]{1,0:T(8,128)(2,1)}, bf16[128,2048]{1,0:T(8,128)(2,1)}, bf16[16,1536]{1,0:T(8,128)(2,1)}) custom-call(s32[10]{0:T(128)} %pad_add_fusion.lens_ref, bf16[256,512]{1,0:T(8,128)(2,1)} %get-tuple-element.40.refs_0_, bf16[256,512]{1,0:T(8,128)(2,1)} %get-tuple-element.42.refs_1_, ...), custom_call_target="tpu_custom_call" | custom-call | flops 1 | bytes 1 | tf_op jit(solution)/shard_map/pallas_call | solution.py:272
  182.1 5.6 %collective-permute-done.6.refs_1_ = bf16[256,2048]{1,0:T(8,128)(2,1)S(1)} collective-permute-done((bf16[256,2048]{1,0:T(8,128)(2,1)S(1)}, bf16[256,2048]{1,0:T(8,128)(2,1)S(1)}, u32[]{:S(2)}, u32[]{:S(2)}) %collective-permute-start.6) | collective-permute-done | bytes 1048608 | tf_op jit(solution)/shard_map/ppermute | solution.py:23
  197.0 7.9 %shard_map.222.refs_4_ = bf16[16,2048]{1,0:T(8,128)(2,1)} custom-call(s32[10]{0:T(128)} %pad_add_fusion.lens_ref, bf16[16,1536]{1,0:T(8,128)(2,1)} %get-tuple-element.58.refs_0_, bf16[16,1536]{1,0:T(8,128)(2,1)} %get-tuple-element.59.refs_1_, bf16[512,2048]{1,0:T(8,128)(2,1)} %refs_2_.3, bf16[8,2048,256]{2,1,0:T(8,128)(2,1)} %refs_3_.3, ...), custom_call_target="tpu_custom_call" | custom-call | flops 1 | bytes 1 | tf_op jit(solution)/shard_map/pallas_call | solution.py:400
  207.7 13.6 %collective-permute-done.10.refs_0_ = bf16[256,2048]{1,0:T(8,128)(2,1)S(1)} collective-permute-done((bf16[256,2048]{1,0:T(8,128)(2,1)S(1)}, bf16[256,2048]{1,0:T(8,128)(2,1)S(1)}, u32[]{:S(2)}, u32[]{:S(2)}) %collective-permute-start.10) | collective-permute-done | bytes 1048608 | tf_op jit(solution)/shard_map/ppermute | solution.py:23
  228.9 8.7 %shard_map.223.refs_5_.refs_1_ = f32[256,2048]{1,0:T(8,128)} custom-call(bf16[256,2048]{1,0:T(8,128)(2,1)} %copy-done.6, bf16[2048,768]{1,0:T(8,128)(2,1)} %refs_5_.1, bf16[2048,768]{1,0:T(8,128)(2,1)} %refs_6_.9, bf16[768,2048]{1,0:T(8,128)(2,1)} %refs_7_.9, bf16[16,2048]{1,0:T(8,128)(2,1)} %shard_map.222.refs_4_), custom_call_target="tpu_custom_call" | custom-call | flops 1 | bytes 1 | tf_op jit(solution)/shard_map/pallas_call | solution.py:508
  237.7 10.9 %shard_map.225 = (f32[256,2048]{1,0:T(8,128)}, f32[256,2048]{1,0:T(8,128)}) custom-call(bf16[256,2048]{1,0:T(8,128)(2,1)} %copy-done.14, bf16[256,2048]{1,0:T(8,128)(2,1)} %collective-permute-done.18.refs_1_, bf16[2048,768]{1,0:T(8,128)(2,1)} %refs_5_.1, bf16[2048,768]{1,0:T(8,128)(2,1)} %refs_6_.9, bf16[768,2048]{1,0:T(8,128)(2,1)} %refs_7_.9, ...), custom_call_target="tpu_custom_call" | custom-call | flops 1 | bytes 1 | tf_op jit(solution)/shard_map/pallas_call | solution.py:508
  248.6 8.3 %collective-permute-done.16.refs_3_ = bf16[16,2048]{1,0:T(8,128)(2,1)S(1)} collective-permute-done((bf16[16,2048]{1,0:T(8,128)(2,1)S(1)}, bf16[16,2048]{1,0:T(8,128)(2,1)S(1)}, u32[]{:S(2)}, u32[]{:S(2)}) %collective-permute-start.16) | collective-permute-done | bytes 65568 | tf_op jit(solution)/shard_map/ppermute | solution.py:23
  258.9 8.8 %shard_map.226 = (f32[256,2048]{1,0:T(8,128)}, f32[16,2048]{1,0:T(8,128)}, f32[16,2048]{1,0:T(8,128)}, f32[16,2048]{1,0:T(8,128)}, f32[16,2048]{1,0:T(8,128)}) custom-call(bf16[256,2048]{1,0:T(8,128)(2,1)} %copy-done.12, bf16[16,2048]{1,0:T(8,128)(2,1)} %copy-done.19, bf16[16,2048]{1,0:T(8,128)(2,1)} %copy-done.18, bf16[16,2048]{1,0:T(8,128)(2,1)} %copy-done.22, ...), custom_call_target="tpu_custom_call" | custom-call | flops 1 | bytes 1 | tf_op jit(solution)/shard_map/pallas_call | solution.py:508
  267.7 11.4 %shard_map.227 = (bf16[256,2048]{1,0:T(8,128)(2,1)}, bf16[256,2048]{1,0:T(8,128)(2,1)}) custom-call(bf16[256,2048]{1,0:T(8,128)(2,1)} %copy-done.14, bf16[256,2048]{1,0:T(8,128)(2,1)} %collective-permute-done.18.refs_1_, f32[256,2048]{1,0:T(8,128)} %get-tuple-element.60.refs_8_.refs_2_, f32[256,2048]{1,0:T(8,128)} %get-tuple-element.66.refs_3_, ...), custom_call_target="tpu_custom_call" | custom-call | flops 1 | bytes 1 | tf_op jit(solution)/shard_map/pallas_call | solution.py:508
  279.5 5.9 %collective-permute-start.19 = (bf16[256,2048]{1,0:T(8,128)(2,1)}, bf16[256,2048]{1,0:T(8,128)(2,1)S(1)}, u32[]{:S(2)}, u32[]{:S(2)}) collective-permute-start(bf16[256,2048]{1,0:T(8,128)(2,1)} %get-tuple-element.67.refs_13_), channel_id=1, source_target_pairs={{0,4},{4,0},{8,12},{12,8},{16,20},{20,16},{24,28},{28,24},{1,5},{5... | collective-permute-start | bytes 3145736 | tf_op jit(solution)/shard_map/ppermute | solution.py:23
  285.4 9.3 %shard_map.228 = (bf16[256,2048]{1,0:T(8,128)(2,1)}, f32[16,2048]{1,0:T(8,128)}, bf16[16,2048]{1,0:T(8,128)(2,1)}, bf16[16,2048]{1,0:T(8,128)(2,1)}, bf16[16,2048]{1,0:T(8,128)(2,1)}) custom-call(bf16[256,2048]{1,0:T(8,128)(2,1)} %copy-done.12, bf16[16,2048]{1,0:T(8,128)(2,1)} %copy-done.19, bf16[16,2048]{1,0:T(8,128)(2,1)} %copy-done.18, ...), custom_call_target="tpu_custom_call" | custom-call | flops 1 | bytes 1 | tf_op jit(solution)/shard_map/pallas_call | solution.py:508
  298.3 7.1 %collective-permute-done.20 = bf16[256,2048]{1,0:T(8,128)(2,1)S(1)} collective-permute-done((bf16[256,2048]{1,0:T(8,128)(2,1)}, bf16[256,2048]{1,0:T(8,128)(2,1)S(1)}, u32[]{:S(2)}, u32[]{:S(2)}) %collective-permute-start.20) | collective-permute-done | bytes 1048608 | tf_op jit(solution)/shard_map/ppermute | solution.py:23
  305.4 5.7 %collective-permute-start.24 = (bf16[16,2048]{1,0:T(8,128)(2,1)}, bf16[16,2048]{1,0:T(8,128)(2,1)S(1)}, u32[]{:S(2)}, u32[]{:S(2)}) collective-permute-start(bf16[16,2048]{1,0:T(8,128)(2,1)} %get-tuple-element.73), channel_id=1, source_target_pairs={{0,12},{4,8},{8,4},{12,0},{16,28},{20,24},{24,20},{28,16},{1,13},{... | collective-permute-start | bytes 196616 | tf_op jit(solution)/shard_map/ppermute | solution.py:23
  311.7 20.5 %collective-permute-done.19 = bf16[256,2048]{1,0:T(8,128)(2,1)S(1)} collective-permute-done((bf16[256,2048]{1,0:T(8,128)(2,1)}, bf16[256,2048]{1,0:T(8,128)(2,1)S(1)}, u32[]{:S(2)}, u32[]{:S(2)}) %collective-permute-start.19) | collective-permute-done | bytes 1048608 | tf_op jit(solution)/shard_map/ppermute | solution.py:23
  333.8 8.8 %shard_map.229.refs_1_ = f32[256,2048]{1,0:T(8,128)} custom-call(bf16[256,2048]{1,0:T(8,128)(2,1)} %copy-done.6, f32[256,2048]{1,0:T(8,128)} %shard_map.223.refs_5_.refs_1_, bf16[4,768,1536]{2,1,0:T(8,128)(2,1)} %bitcast.31, bf16[4,768,1536]{2,1,0:T(8,128)(2,1)} %bitcast.32, bf16[4,768,1536]{2,1,0:T(8,128)(2,1)} %bitcast.33, ...), custom_call_target="tpu_custom_call" | custom-call | flops 1 | bytes 1 | tf_op jit(solution)/shard_map/pallas_call | solution.py:508
  366.5 9.6 %convolution_reduce_fusion = f32[128]{0:T(128)S(1)} fusion(bf16[128,2048]{1,0:T(8,128)(2,1)} %shard_map.231, bf16[2048,4748]{0,1:T(8,128)(2,1)} %param.41), kind=kOutput, calls=%fused_computation.14 | convolution fusion | flops 2489927168 | bytes 19972608 | tf_op jit(solution)/shard_map/dot_general | solution.py:533
  (175 shorter events, 95.1 us)
Async XLA Ops:
  10.4 84.1 %all-to-all-start = ((bf16[32,8,2048]{2,1,0:T(8,128)(2,1)}), bf16[32,8,2048]{2,1,0:T(8,128)(2,1)S(1)}, u32[]{:S(2)}, u32[]{:S(2)}) async-start(bf16[32,8,2048]{2,1,0:T(8,128)(2,1)} %bitcast.3), calls=%async_computation | async-start | bytes 2097152 | tf_op jit(solution)/shard_map/all_to_all | solution.py:529
  20.9 100.8 %collective-permute-start.2 = (bf16[768,1536]{1,0:T(8,128)(2,1)}, bf16[768,1536]{1,0:T(8,128)(2,1)}, u32[]{:S(2)}, u32[]{:S(2)}) collective-permute-start(bf16[768,1536]{1,0:T(8,128)(2,1)} %shard_map.215), channel_id=1, source_target_pairs={{0,8},{4,12},{8,16},{12,20},{16,24},{20,28},{24,0},{28,4},{1,9},{5... | collective-permute-start | bytes 7077896 | tf_op jit(solution)/shard_map/ppermute | solution.py:617
  95.0 9.4 %collective-permute-start = (bf16[256,2048]{1,0:T(8,128)(2,1)S(1)}, bf16[256,2048]{1,0:T(8,128)(2,1)}, u32[]{:S(2)}, u32[]{:S(2)}) collective-permute-start(bf16[256,2048]{1,0:T(8,128)(2,1)S(1)} %convolution_convert_fusion.2.refs_0_.refs_9_), channel_id=1, source_target_pairs={{0,1},{1,0},{2,3},{3,2},{4,5},{5,4},{6,7},{7,6},{8,9},{9,8},{10,11... | collective-permute-start | bytes 3145736 | tf_op jit(solution)/shard_map/ppermute | solution.py:23
  95.1 25.6 %collective-permute-start.1 = (bf16[256,2048]{1,0:T(8,128)(2,1)S(1)}, bf16[256,2048]{1,0:T(8,128)(2,1)S(1)}, u32[]{:S(2)}, u32[]{:S(2)}) collective-permute-start(bf16[256,2048]{1,0:T(8,128)(2,1)S(1)} %convolution_convert_fusion.2.refs_0_.refs_9_), channel_id=1, source_target_pairs={{0,2},{1,3},{2,0},{3,1},{4,6},{5,7},{6,4},{7,5},{8,10},{9,11},{10,... | collective-permute-start | bytes 3145736 | tf_op jit(solution)/shard_map/ppermute | solution.py:23
  121.7 8.0 %collective-permute-start.3 = (bf16[256,2048]{1,0:T(8,128)(2,1)}, bf16[256,2048]{1,0:T(8,128)(2,1)S(1)}, u32[]{:S(2)}, u32[]{:S(2)}) collective-permute-start(bf16[256,2048]{1,0:T(8,128)(2,1)} %shard_map.214.refs_0_), channel_id=1, source_target_pairs={{0,1},{1,0},{2,3},{3,2},{4,5},{5,4},{6,7},{7,6},{8,9},{9,8},{10,11... | collective-permute-start | bytes 3145736 | tf_op jit(solution)/shard_map/ppermute | solution.py:23
  121.7 60.4 %collective-permute-start.7 = (bf16[768,1536]{1,0:T(8,128)(2,1)}, bf16[768,1536]{1,0:T(8,128)(2,1)S(1)}, u32[]{:S(2)}, u32[]{:S(2)}) collective-permute-start(bf16[768,1536]{1,0:T(8,128)(2,1)} %collective-permute-done.2.refs_9_), channel_id=1, source_target_pairs={{0,8},{4,12},{8,16},{12,20},{16,24},{20,28},{24,0},{28,4},{1,9},{5... | collective-permute-start | bytes 7077896 | tf_op jit(solution)/shard_map/ppermute | solution.py:617
  162.4 25.4 %collective-permute-start.6 = (bf16[256,2048]{1,0:T(8,128)(2,1)S(1)}, bf16[256,2048]{1,0:T(8,128)(2,1)S(1)}, u32[]{:S(2)}, u32[]{:S(2)}) collective-permute-start(bf16[256,2048]{1,0:T(8,128)(2,1)S(1)} %add_convert_fusion.1.refs_13_), channel_id=1, source_target_pairs={{0,2},{1,3},{2,0},{3,1},{4,6},{5,7},{6,4},{7,5},{8,10},{9,11},{10,... | collective-permute-start | bytes 3145736 | tf_op jit(solution)/shard_map/ppermute | solution.py:23
  188.7 79.0 %all-gather.3.cloned.1.call-start = ((), (), s32[]{:S(2)}) async-start(), calls=%async_computation.2 | async-start | bytes 11796480 | tf_op jit(solution)/shard_map/all_gather | solution.py:664
  196.0 25.3 %collective-permute-start.10 = (bf16[256,2048]{1,0:T(8,128)(2,1)S(1)}, bf16[256,2048]{1,0:T(8,128)(2,1)S(1)}, u32[]{:S(2)}, u32[]{:S(2)}) collective-permute-start(bf16[256,2048]{1,0:T(8,128)(2,1)S(1)} %fusion.3.refs_5_.refs_0_), channel_id=1, source_target_pairs={{0,4},{4,0},{8,12},{12,8},{16,20},{20,16},{24,28},{28,24},{1,5},{5... | collective-permute-start | bytes 3145736 | tf_op jit(solution)/shard_map/ppermute | solution.py:23
  204.9 16.4 %collective-permute-start.14 = (bf16[16,2048]{1,0:T(8,128)(2,1)}, bf16[16,2048]{1,0:T(8,128)(2,1)S(1)}, u32[]{:S(2)}, u32[]{:S(2)}) collective-permute-start(bf16[16,2048]{1,0:T(8,128)(2,1)} %shard_map.222.refs_4_), channel_id=1, source_target_pairs={{0,3},{1,2},{2,1},{3,0},{4,7},{5,6},{6,5},{7,4},{8,11},{9,10},{10,... | collective-permute-start | bytes 196616 | tf_op jit(solution)/shard_map/ppermute | solution.py:23
  205.0 16.3 %collective-permute-start.13 = (bf16[16,2048]{1,0:T(8,128)(2,1)}, bf16[16,2048]{1,0:T(8,128)(2,1)S(1)}, u32[]{:S(2)}, u32[]{:S(2)}) collective-permute-start(bf16[16,2048]{1,0:T(8,128)(2,1)} %shard_map.222.refs_4_), channel_id=1, source_target_pairs={{0,2},{1,3},{2,0},{3,1},{4,6},{5,7},{6,4},{7,5},{8,10},{9,11},{10,... | collective-permute-start | bytes 196616 | tf_op jit(solution)/shard_map/ppermute | solution.py:23
  206.8 14.5 %collective-permute-start.12 = (bf16[16,2048]{1,0:T(8,128)(2,1)}, bf16[16,2048]{1,0:T(8,128)(2,1)S(1)}, u32[]{:S(2)}, u32[]{:S(2)}) collective-permute-start(bf16[16,2048]{1,0:T(8,128)(2,1)} %shard_map.222.refs_4_), channel_id=1, source_target_pairs={{0,1},{1,0},{2,3},{3,2},{4,5},{5,4},{6,7},{7,6},{8,9},{9,8},{10,11... | collective-permute-start | bytes 196616 | tf_op jit(solution)/shard_map/ppermute | solution.py:23
  206.9 30.8 %collective-permute-start.18 = (bf16[256,2048]{1,0:T(8,128)(2,1)}, bf16[256,2048]{1,0:T(8,128)(2,1)}, u32[]{:S(2)}, u32[]{:S(2)}) collective-permute-start(bf16[256,2048]{1,0:T(8,128)(2,1)} %copy-done.6), channel_id=1, source_target_pairs={{0,8},{4,12},{8,0},{12,4},{16,24},{20,28},{24,16},{28,20},{1,9},{5... | collective-permute-start | bytes 3145736 | tf_op jit(solution)/shard_map/ppermute | solution.py:23
  221.3 36.6 %collective-permute-start.11 = (bf16[256,2048]{1,0:T(8,128)(2,1)S(1)}, bf16[256,2048]{1,0:T(8,128)(2,1)S(1)}, u32[]{:S(2)}, u32[]{:S(2)}) collective-permute-start(bf16[256,2048]{1,0:T(8,128)(2,1)S(1)} %collective-permute-done.10.refs_0_), channel_id=1, source_target_pairs={{0,8},{4,12},{8,0},{12,4},{16,24},{20,28},{24,16},{28,20},{1,9},{5... | collective-permute-start | bytes 3145736 | tf_op jit(solution)/shard_map/ppermute | solution.py:23
  223.2 33.7 %collective-permute-start.16 = (bf16[16,2048]{1,0:T(8,128)(2,1)S(1)}, bf16[16,2048]{1,0:T(8,128)(2,1)S(1)}, u32[]{:S(2)}, u32[]{:S(2)}) collective-permute-start(bf16[16,2048]{1,0:T(8,128)(2,1)S(1)} %fusion.15.refs_1_), channel_id=1, source_target_pairs={{0,8},{4,12},{8,0},{12,4},{16,24},{20,28},{24,16},{28,20},{1,9},{5... | collective-permute-start | bytes 196616 | tf_op jit(solution)/shard_map/ppermute | solution.py:23
  227.2 30.7 %collective-permute-start.17 = (bf16[16,2048]{1,0:T(8,128)(2,1)S(1)}, bf16[16,2048]{1,0:T(8,128)(2,1)S(1)}, u32[]{:S(2)}, u32[]{:S(2)}) collective-permute-start(bf16[16,2048]{1,0:T(8,128)(2,1)S(1)} %collective-permute-done.15.refs_6_.refs_2_), channel_id=1, source_target_pairs={{0,8},{4,12},{8,0},{12,4},{16,24},{20,28},{24,16},{28,20},{1,9},{5... | collective-permute-start | bytes 196616 | tf_op jit(solution)/shard_map/ppermute | solution.py:23
  279.1 26.3 %collective-permute-start.20 = (bf16[256,2048]{1,0:T(8,128)(2,1)}, bf16[256,2048]{1,0:T(8,128)(2,1)S(1)}, u32[]{:S(2)}, u32[]{:S(2)}) collective-permute-start(bf16[256,2048]{1,0:T(8,128)(2,1)} %get-tuple-element.69), channel_id=1, source_target_pairs={{0,8},{4,12},{8,0},{12,4},{16,24},{20,28},{24,16},{28,20},{1,9},{5... | collective-permute-start | bytes 3145736 | tf_op jit(solution)/shard_map/ppermute | solution.py:23
  279.5 52.7 %collective-permute-start.19 = (bf16[256,2048]{1,0:T(8,128)(2,1)}, bf16[256,2048]{1,0:T(8,128)(2,1)S(1)}, u32[]{:S(2)}, u32[]{:S(2)}) collective-permute-start(bf16[256,2048]{1,0:T(8,128)(2,1)} %get-tuple-element.67.refs_13_), channel_id=1, source_target_pairs={{0,4},{4,0},{8,12},{12,8},{16,20},{20,16},{24,28},{28,24},{1,5},{5... | collective-permute-start | bytes 3145736 | tf_op jit(solution)/shard_map/ppermute | solution.py:23
  294.7 51.7 %collective-permute-start.21 = (bf16[256,2048]{1,0:T(8,128)(2,1)}, bf16[256,2048]{1,0:T(8,128)(2,1)}, u32[]{:S(2)}, u32[]{:S(2)}) collective-permute-start(bf16[256,2048]{1,0:T(8,128)(2,1)} %get-tuple-element.68.refs_5_), channel_id=1, source_target_pairs={{0,12},{4,8},{8,4},{12,0},{16,28},{20,24},{24,20},{28,16},{1,13},{... | collective-permute-start | bytes 3145736 | tf_op jit(solution)/shard_map/ppermute | solution.py:23
  296.0 46.6 %collective-permute-start.22 = (bf16[16,2048]{1,0:T(8,128)(2,1)}, bf16[16,2048]{1,0:T(8,128)(2,1)S(1)}, u32[]{:S(2)}, u32[]{:S(2)}) collective-permute-start(bf16[16,2048]{1,0:T(8,128)(2,1)} %get-tuple-element.71), channel_id=1, source_target_pairs={{0,4},{4,0},{8,12},{12,8},{16,20},{20,16},{24,28},{28,24},{1,5},{5... | collective-permute-start | bytes 196616 | tf_op jit(solution)/shard_map/ppermute | solution.py:23
  298.0 44.6 %collective-permute-start.23 = (bf16[16,2048]{1,0:T(8,128)(2,1)}, bf16[16,2048]{1,0:T(8,128)(2,1)S(1)}, u32[]{:S(2)}, u32[]{:S(2)}) collective-permute-start(bf16[16,2048]{1,0:T(8,128)(2,1)} %get-tuple-element.72), channel_id=1, source_target_pairs={{0,8},{4,12},{8,0},{12,4},{16,24},{20,28},{24,16},{28,20},{1,9},{5... | collective-permute-start | bytes 196616 | tf_op jit(solution)/shard_map/ppermute | solution.py:23
  305.4 37.2 %collective-permute-start.24 = (bf16[16,2048]{1,0:T(8,128)(2,1)}, bf16[16,2048]{1,0:T(8,128)(2,1)S(1)}, u32[]{:S(2)}, u32[]{:S(2)}) collective-permute-start(bf16[16,2048]{1,0:T(8,128)(2,1)} %get-tuple-element.73), channel_id=1, source_target_pairs={{0,12},{4,8},{8,4},{12,0},{16,28},{20,24},{24,20},{28,16},{1,13},{... | collective-permute-start | bytes 196616 | tf_op jit(solution)/shard_map/ppermute | solution.py:23
  354.8 10.8 %collective-permute-start.27 = (bf16[64,2048]{1,0:T(8,128)(2,1)S(1)}, bf16[64,2048]{1,0:T(8,128)(2,1)S(1)}, u32[]{:S(2)}, u32[]{:S(2)}) collective-permute-start(bf16[64,2048]{1,0:T(8,128)(2,1)S(1)} %pad_maximum_fusion.4), channel_id=1, source_target_pairs={{0,16},{4,20},{8,24},{12,28},{16,0},{20,4},{24,8},{28,12},{1,17},{... | collective-permute-start | bytes 786440 | tf_op jit(solution)/shard_map/ppermute | solution.py:23
  360.0 33.2 %all-to-all-start.1 = ((bf16[32,8,2048]{2,1,0:T(8,128)(2,1)}), bf16[32,8,2048]{2,1,0:T(8,128)(2,1)S(1)}, u32[]{:S(2)}, u32[]{:S(2)}) async-start(bf16[32,8,2048]{2,1,0:T(8,128)(2,1)} %fusion), calls=%async_computation.1 | async-start | bytes 2097152 | tf_op jit(solution)/shard_map/all_to_all | solution.py:529
  (39 other events, 198.1 us)
Sparse Core Ops, SparseCore 0:
  191.1 65.8 all-gather.2

commit v2 on v1

--- a/solution.py
+++ b/solution.py
@@ -608,16 +608,16 @@
 
     send_hot, slot_hot = routes(slot_tokens, self_index, devices, rows_dev, ready)
     sent = pick(send_hot, hidden_in)
+    arrived = regroup(sent)
+    owner_rows = pick(slot_hot, arrived)
     far_count = req_count // GROUP
-    far_share = share_of(kv_index[None], width // kv_count, w_gate, w_up, w_down, sent)
+    far_share = share_of(kv_index[None], width // kv_count, w_gate, w_up, w_down, arrived)
     step = GROUP if far_count > 2 else GROUP // 2
     ring = [(i, (i + step) % req_count) for i in range(req_count)]
     far_hops = [far_share]
     for _ in range(max(2, far_count - 1)):
         far_hops.append(lax.ppermute(far_hops[-1], "req", ring))
     far_shares = far_hops[GROUP // step :]
-    arrived = regroup(sent)
-    owner_rows = pick(slot_hot, arrived)
 
     def project_block(diff, follows):
         block_at = (kv_index ^ diff) * rows_dev
@@ -634,7 +634,7 @@
         blocks[diff] = pin(even[diff], parts[1][2])
         blocks[diff + 1] = swap(blocks[diff], "kv", 1)
     for diff in range(2, kv_count):
-        parts.append(project_block(diff, far_hops[1] if diff == 2 else parts[-1][2]))
+        parts.append(project_block(diff, parts[-1][2]))
 
     f32, bf16 = jnp.float32, jnp.bfloat16
     lens = jnp.concatenate([kv_index[None], prefill_start, cache_len]).astype(jnp.int32)
@@ -652,17 +652,15 @@
             follows,
         )
         if pair:
-            other = jnp.concatenate([swap(half, "kv", 1) for half in sum_odd], axis=0)
+            halves = [swap(pin(half, far_hops[1]), "kv", 1) for half in sum_odd]
+            other = jnp.concatenate(halves, axis=0)
             both = sum_even.astype(f32) + other.astype(f32)
             follows = both.astype(bf16)
             sums.append(swap(follows, "kv", 2 * pair))
         else:
-            halves = [swap(pin(half, *sums, *far_shares), "kv", 1) for half in sum_odd]
+            halves = [swap(pin(half, *sums), "kv", 1) for half in sum_odd]
             sums.append(jnp.concatenate(halves, axis=0))
             own_sum = sum_even
-    far_weights = [
-        lax.all_gather(pin(held, own_sum), "kv") for held in far_shares
-    ]
     resid = owner_rows.astype(f32) + own_sum
     for each in sums:
         resid = resid + each.astype(f32)
@@ -682,6 +680,9 @@
         value_cache,
         ffn_in,
     )
+    far_weights = [
+        lax.all_gather(pin(held, last_sum), "kv") for held in far_shares
+    ]
     last_raw = blocks[0][rows_dev - TAIL :]
     for diff in range(1, kv_count):
         is_last = (kv_index ^ diff) == kv_count - 1
@@ -704,8 +705,8 @@
         [near[3], *lasts_in], [bf16, f32] + [bf16] * (GROUP - 1), far_weights, [first], rest
     )
     backs = [swap(first, "req", 1), swap(second, "req", 2), swap(third, "req", 3)]
-    (own_part,) = feed_forward([ffn_in], [f32], far_weights, [third, backs[0][:TAIL], backs[1][:TAIL]], zero)
-    last_part = pin(last_part, own_part)
+    (own_part,) = feed_forward([ffn_in], [f32], far_weights, [third], zero)
+    last_part = pin(last_part, own_part, backs[0][:TAIL], backs[1][:TAIL])
     for diff, part in enumerate(last_parts, 1):
         last_part = last_part + swap(part, "req", diff).astype(f32)
     last_rows = (last_resid.astype(f32) + last_part).astype(bf16)

time: 409 us -> 365 us (0.89)
  waiting for transfers between devices: 156 us -> 121 us
  starting transfers between devices: 51 us -> 38.3 us
    all_to_all x2, waiting for transfers between devices: 65.3 us -> 19 us  [regroup(): lax.all_to_all(rows_in, ('req', 'kv'), split_axis=0, concat_axis=0, tiled...]
    ppermute x31, starting transfers between devices: 37.8 us -> 23.7 us  [swap(): return lax.ppermute(value, axis, [(i, i ^ bit) for i in range(size)])]
    ppermute x2, waiting for transfers between devices: 0.01 us -> 13.4 us  [shards(): far_hops.append(lax.ppermute(far_hops[-1], 'req', ring))]
    unnamed x54 -> x50, local copies, waits for them, and re-layouts: 8.3 us -> 9.49 us
  transfers between devices with their start and end apart: 36 -> 36, of which waited for: 20 -> 23; matrix products, arithmetic and copies ran while one was open for 8% -> 9% of each run, Pallas kernels for 30% -> 33%
where the time goes in v2:
time: 365 us; the launch traced here: 359 us
  Pallas kernels  132 us (36%)
  waiting for transfers between devices  121 us (33%)
  starting transfers between devices  38.3 us (10%)
  between operations  18.2 us (5%)
  local copies, waits for them, and re-layouts  16.7 us (5%)
  matrix products  16 us (4%)
  other arithmetic  16 us (4%)
    ppermute x31, waiting for transfers between devices, swap(): return lax.ppermute(value, axis, [(i, i ^ bit) for i in range(size)])  88.6 us
    pallas_call x6, Pallas kernels, feed_forward(): pl.pallas_call(kernel, out_shape=[jax.ShapeDtypeStruct((count, width), dt...  57.2 us
    pallas_call x2, Pallas kernels, attend(): pl.pallas_call(functools.partial(attend_kernel, pair, block_count, head_d...  39.8 us
    pallas_call x4, Pallas kernels, project(): pl.pallas_call(functools.partial(project_kernel, len(blocks), head_dim),...  24.5 us
    ppermute x31, starting transfers between devices, swap(): return lax.ppermute(value, axis, [(i, i ^ bit) for i in range(size)])  23.7 us
    all_to_all x2, waiting for transfers between devices, regroup(): lax.all_to_all(rows_in, ('req', 'kv'), split_axis=0, concat_axis=0, tiled...  19 us
    all_to_all x2, starting transfers between devices, regroup(): lax.all_to_all(rows_in, ('req', 'kv'), split_axis=0, concat_axis=0, tiled...  13.5 us
    ppermute x2, waiting for transfers between devices, shards(): far_hops.append(lax.ppermute(far_hops[-1], 'req', ring))  13.4 us
  transfers between devices with their start and end apart: 36, of which 23 were waited for; matrix products, arithmetic and copies ran while one was open for 9% of the time, Pallas kernels for 33%

profile of v2, /device:TPU:0, one launch (start us, length us, event | category | flops | bytes accessed | tf_op | source)
XLA Modules:
  0.0 358.6 jit_solution(5964279527522594644)
XLA Ops:
  10.4 7.3 %all-to-all-start = ((bf16[32,8,2048]{2,1,0:T(8,128)(2,1)}), bf16[32,8,2048]{2,1,0:T(8,128)(2,1)S(1)}, u32[]{:S(2)}, u32[]{:S(2)}) async-start(bf16[32,8,2048]{2,1,0:T(8,128)(2,1)} %fusion), calls=%async_computation | async-start | bytes 2097152 | tf_op jit(solution)/shard_map/all_to_all | solution.py:529
  25.0 19.0 %all-to-all-done = bf16[32,8,2048]{2,1,0:T(8,128)(2,1)S(1)} async-done(((bf16[32,8,2048]{2,1,0:T(8,128)(2,1)}), bf16[32,8,2048]{2,1,0:T(8,128)(2,1)S(1)}, u32[]{:S(2)}, u32[]{:S(2)}) %all-to-all-start) | async-done | bytes 1048608 | tf_op jit(solution)/shard_map/all_to_all | solution.py:529
  53.9 6.1 %shard_map.212 = (bf16[256,512]{1,0:T(8,128)(2,1)}, bf16[256,256]{1,0:T(8,128)(2,1)}, bf16[256,256]{1,0:T(8,128)(2,1)}) custom-call(bf16[256,2048]{1,0:T(8,128)(2,1)} %copy-done.3, f32[1,2048]{1,0:T(1,128)} %bitcast.40, f32[256,128]{1,0:T(8,128)} %get-tuple-element.87.refs_2_, f32[256,128]{1,0:T(8,128)} %get-tuple-element.83.refs_3_, f32[1,128]{1,0:T(1,128)} %bitcast.46, ...), custom_call_target="tpu_custom_call" | custom-call | flops 1 | bytes 1 | tf_op jit(solution)/shard_map/pallas_call | solution.py:116
  60.0 6.1 %shard_map.213 = (bf16[256,512]{1,0:T(8,128)(2,1)}, bf16[256,256]{1,0:T(8,128)(2,1)}, bf16[256,256]{1,0:T(8,128)(2,1)}) custom-call(bf16[256,2048]{1,0:T(8,128)(2,1)} %collective-permute-done.refs_0_, f32[1,2048]{1,0:T(1,128)} %bitcast.41, f32[256,128]{1,0:T(8,128)} %get-tuple-element.86.refs_2_, f32[256,128]{1,0:T(8,128)} %get-tuple-element.82.refs_3_, ...), custom_call_target="tpu_custom_call" | custom-call | flops 1 | bytes 1 | tf_op jit(solution)/shard_map/pallas_call | solution.py:116
  66.2 10.2 %collective-permute-done.1.refs_0_ = bf16[256,2048]{1,0:T(8,128)(2,1)S(1)} collective-permute-done((bf16[256,2048]{1,0:T(8,128)(2,1)S(1)}, bf16[256,2048]{1,0:T(8,128)(2,1)S(1)}, u32[]{:S(2)}, u32[]{:S(2)}) %collective-permute-start.1) | collective-permute-done | bytes 1048608 | tf_op jit(solution)/shard_map/ppermute | solution.py:23
  78.1 6.1 %shard_map.215 = (bf16[256,512]{1,0:T(8,128)(2,1)}, bf16[256,256]{1,0:T(8,128)(2,1)}, bf16[256,256]{1,0:T(8,128)(2,1)}) custom-call(bf16[256,2048]{1,0:T(8,128)(2,1)} %shard_map.214.refs_0_, f32[1,2048]{1,0:T(1,128)} %bitcast.42, f32[256,128]{1,0:T(8,128)} %get-tuple-element.85.refs_2_, f32[256,128]{1,0:T(8,128)} %get-tuple-element.81.refs_3_, ...), custom_call_target="tpu_custom_call" | custom-call | flops 1 | bytes 1 | tf_op jit(solution)/shard_map/pallas_call | solution.py:116
  85.2 6.1 %shard_map.216 = (bf16[256,512]{1,0:T(8,128)(2,1)}, bf16[256,256]{1,0:T(8,128)(2,1)}, bf16[256,256]{1,0:T(8,128)(2,1)}) custom-call(bf16[256,2048]{1,0:T(8,128)(2,1)} %copy-done.15, f32[1,2048]{1,0:T(1,128)} %bitcast.43, f32[256,128]{1,0:T(8,128)} %get-tuple-element.84.refs_2_, f32[256,128]{1,0:T(8,128)} %get-tuple-element.80.refs_3_, f32[1,128]{1,0:T(1,128)} %bitcast.49, ...), custom_call_target="tpu_custom_call" | custom-call | flops 1 | bytes 1 | tf_op jit(solution)/shard_map/pallas_call | solution.py:116
  91.4 21.2 %shard_map.217 = (bf16[256,2048]{1,0:T(8,128)(2,1)}, bf16[128,2048]{1,0:T(8,128)(2,1)}, bf16[128,2048]{1,0:T(8,128)(2,1)}, bf16[16,1536]{1,0:T(8,128)(2,1)}) custom-call(s32[10]{0:T(128)} %pad_add_fusion.lens_ref, bf16[256,512]{1,0:T(8,128)(2,1)} %get-tuple-element.50.refs_0_, bf16[256,512]{1,0:T(8,128)(2,1)} %get-tuple-element.51.refs_1_, ...), custom_call_target="tpu_custom_call" | custom-call | flops 1 | bytes 1 | tf_op jit(solution)/shard_map/pallas_call | solution.py:272
  117.1 18.7 %shard_map.221 = (f32[256,2048]{1,0:T(8,128)}, bf16[128,2048]{1,0:T(8,128)(2,1)}, bf16[128,2048]{1,0:T(8,128)(2,1)}, bf16[16,1536]{1,0:T(8,128)(2,1)}) custom-call(s32[10]{0:T(128)} %pad_add_fusion.lens_ref, bf16[256,512]{1,0:T(8,128)(2,1)} %get-tuple-element.40.refs_0_, bf16[256,512]{1,0:T(8,128)(2,1)} %get-tuple-element.42.refs_1_, ...), custom_call_target="tpu_custom_call" | custom-call | flops 1 | bytes 1 | tf_op jit(solution)/shard_map/pallas_call | solution.py:272
  135.7 5.8 %collective-permute-done.6.refs_1_ = bf16[256,2048]{1,0:T(8,128)(2,1)S(1)} collective-permute-done((bf16[256,2048]{1,0:T(8,128)(2,1)S(1)}, bf16[256,2048]{1,0:T(8,128)(2,1)S(1)}, u32[]{:S(2)}, u32[]{:S(2)}) %collective-permute-start.6) | collective-permute-done | bytes 1048608 | tf_op jit(solution)/shard_map/ppermute | solution.py:23
  150.6 7.8 %shard_map.224.refs_4_.refs_1_ = bf16[16,2048]{1,0:T(8,128)(2,1)} custom-call(s32[10]{0:T(128)} %pad_add_fusion.lens_ref, bf16[16,1536]{1,0:T(8,128)(2,1)} %get-tuple-element.58.refs_0_, bf16[16,1536]{1,0:T(8,128)(2,1)} %get-tuple-element.59.refs_1_, bf16[512,2048]{1,0:T(8,128)(2,1)} %refs_2_.3, bf16[8,2048,256]{2,1,0:T(8,128)(2,1)} %refs_3_.3, ...), custom_call_target="tpu_custom_call" | custom-call | flops 1 | bytes 1 | tf_op jit(solution)/shard_map/pallas_call | solution.py:400
  158.4 13.4 %collective-permute-done.9.refs_0_ = bf16[768,1536]{1,0:T(8,128)(2,1)S(1)} collective-permute-done((bf16[768,1536]{1,0:T(8,128)(2,1)}, bf16[768,1536]{1,0:T(8,128)(2,1)S(1)}, u32[]{:S(2)}, u32[]{:S(2)}) %collective-permute-start.9) | collective-permute-done | bytes 2359328 | tf_op jit(solution)/shard_map/ppermute | solution.py:619
  176.2 22.9 %collective-permute-done.10.refs_0_ = bf16[256,2048]{1,0:T(8,128)(2,1)} collective-permute-done((bf16[256,2048]{1,0:T(8,128)(2,1)S(1)}, bf16[256,2048]{1,0:T(8,128)(2,1)}, u32[]{:S(2)}, u32[]{:S(2)}) %collective-permute-start.10) | collective-permute-done | bytes 1048608 | tf_op jit(solution)/shard_map/ppermute | solution.py:23
  206.7 8.4 %shard_map.225.refs_5_.refs_1_ = f32[256,2048]{1,0:T(8,128)} custom-call(bf16[256,2048]{1,0:T(8,128)(2,1)} %fusion.4.refs_5_.refs_0_, bf16[2048,768]{1,0:T(8,128)(2,1)} %refs_5_.1, bf16[2048,768]{1,0:T(8,128)(2,1)} %refs_6_.9, bf16[768,2048]{1,0:T(8,128)(2,1)} %refs_7_.9, bf16[16,2048]{1,0:T(8,128)(2,1)} %shard_map.224.refs_4_.refs_1_), custom_call_target="tpu_custom_call" | custom-call | flops 1 | bytes 1 | tf_op jit(solution)/shard_map/pallas_call | solution.py:508
  215.1 10.8 %shard_map.227 = (f32[256,2048]{1,0:T(8,128)}, f32[256,2048]{1,0:T(8,128)}) custom-call(bf16[256,2048]{1,0:T(8,128)(2,1)} %collective-permute-done.10.refs_0_, bf16[256,2048]{1,0:T(8,128)(2,1)} %collective-permute-done.18.refs_1_, bf16[2048,768]{1,0:T(8,128)(2,1)} %refs_5_.1, bf16[2048,768]{1,0:T(8,128)(2,1)} %refs_6_.9, bf16[768,2048]{1,0:T(8,128)(2,1)} %refs_7_.9, ...), custom_call_target="tpu_custom_call" | custom-call | flops 1 | bytes 1 | tf_op jit(solution)/shard_map/pallas_call | solution.py:508
  228.0 8.8 %shard_map.228 = (f32[256,2048]{1,0:T(8,128)}, f32[16,2048]{1,0:T(8,128)}, f32[16,2048]{1,0:T(8,128)}, f32[16,2048]{1,0:T(8,128)}, f32[16,2048]{1,0:T(8,128)}) custom-call(bf16[256,2048]{1,0:T(8,128)(2,1)} %copy-done.12, bf16[16,2048]{1,0:T(8,128)(2,1)} %copy-done.19, bf16[16,2048]{1,0:T(8,128)(2,1)} %copy-done.18, bf16[16,2048]{1,0:T(8,128)(2,1)} %copy-done.20, ...), custom_call_target="tpu_custom_call" | custom-call | flops 1 | bytes 1 | tf_op jit(solution)/shard_map/pallas_call | solution.py:508
  236.8 11.4 %shard_map.229 = (bf16[256,2048]{1,0:T(8,128)(2,1)}, bf16[256,2048]{1,0:T(8,128)(2,1)}) custom-call(bf16[256,2048]{1,0:T(8,128)(2,1)} %collective-permute-done.10.refs_0_, bf16[256,2048]{1,0:T(8,128)(2,1)} %collective-permute-done.18.refs_1_, f32[256,2048]{1,0:T(8,128)} %get-tuple-element.60.refs_8_.refs_2_, f32[256,2048]{1,0:T(8,128)} %get-tuple-element.66.refs_3_, ...), custom_call_target="tpu_custom_call" | custom-call | flops 1 | bytes 1 | tf_op jit(solution)/shard_map/pallas_call | solution.py:508
  250.6 9.0 %shard_map.230 = (bf16[256,2048]{1,0:T(8,128)(2,1)}, f32[16,2048]{1,0:T(8,128)}, bf16[16,2048]{1,0:T(8,128)(2,1)}, bf16[16,2048]{1,0:T(8,128)(2,1)}, bf16[16,2048]{1,0:T(8,128)(2,1)}) custom-call(bf16[256,2048]{1,0:T(8,128)(2,1)} %copy-done.12, bf16[16,2048]{1,0:T(8,128)(2,1)} %copy-done.19, bf16[16,2048]{1,0:T(8,128)(2,1)} %copy-done.18, ...), custom_call_target="tpu_custom_call" | custom-call | flops 1 | bytes 1 | tf_op jit(solution)/shard_map/pallas_call | solution.py:508
  263.2 11.9 %collective-permute-done.19 = bf16[256,2048]{1,0:T(8,128)(2,1)S(1)} collective-permute-done((bf16[256,2048]{1,0:T(8,128)(2,1)}, bf16[256,2048]{1,0:T(8,128)(2,1)S(1)}, u32[]{:S(2)}, u32[]{:S(2)}) %collective-permute-start.19) | collective-permute-done | bytes 1048608 | tf_op jit(solution)/shard_map/ppermute | solution.py:23
  276.8 8.7 %shard_map.231.refs_1_ = f32[256,2048]{1,0:T(8,128)} custom-call(bf16[256,2048]{1,0:T(8,128)(2,1)} %fusion.4.refs_5_.refs_0_, f32[256,2048]{1,0:T(8,128)} %shard_map.225.refs_5_.refs_1_, bf16[4,768,1536]{2,1,0:T(8,128)(2,1)} %bitcast.32, bf16[4,768,1536]{2,1,0:T(8,128)(2,1)} %bitcast.33, bf16[4,768,1536]{2,1,0:T(8,128)(2,1)} %bitcast.34, ...), custom_call_target="tpu_custom_call" | custom-call | flops 1 | bytes 1 | tf_op jit(solution)/shard_map/pallas_call | solution.py:508
  288.6 7.2 %collective-permute-done.22 = bf16[16,2048]{1,0:T(8,128)(2,1)S(1)} collective-permute-done((bf16[16,2048]{1,0:T(8,128)(2,1)}, bf16[16,2048]{1,0:T(8,128)(2,1)S(1)}, u32[]{:S(2)}, u32[]{:S(2)}) %collective-permute-start.22) | collective-permute-done | bytes 65568 | tf_op jit(solution)/shard_map/ppermute | solution.py:23
  306.3 4.2 %collective-permute-done.26 = bf16[32,2048]{1,0:T(8,128)(2,1)S(1)} collective-permute-done((bf16[32,2048]{1,0:T(8,128)(2,1)S(1)}, bf16[32,2048]{1,0:T(8,128)(2,1)S(1)}, u32[]{:S(2)}, u32[]{:S(2)}) %collective-permute-start.26) | collective-permute-done | bytes 131104 | tf_op jit(solution)/shard_map/ppermute | solution.py:23
  313.0 6.2 %all-to-all-start.1 = ((bf16[32,8,2048]{2,1,0:T(8,128)(2,1)}), bf16[32,8,2048]{2,1,0:T(8,128)(2,1)S(1)}, u32[]{:S(2)}, u32[]{:S(2)}) async-start(bf16[32,8,2048]{2,1,0:T(8,128)(2,1)} %fusion.1), calls=%async_computation.1 | async-start | bytes 2097152 | tf_op jit(solution)/shard_map/all_to_all | solution.py:529
  323.3 9.6 %convolution_reduce_fusion = f32[128]{0:T(128)S(1)} fusion(bf16[128,2048]{1,0:T(8,128)(2,1)} %shard_map.233, bf16[2048,4748]{0,1:T(8,128)(2,1)} %param.41), kind=kOutput, calls=%fused_computation.15 | convolution fusion | flops 2489927168 | bytes 19972608 | tf_op jit(solution)/shard_map/dot_general | solution.py:533
  (173 shorter events, 93.4 us)
Async XLA Ops:
  10.4 33.5 %all-to-all-start = ((bf16[32,8,2048]{2,1,0:T(8,128)(2,1)}), bf16[32,8,2048]{2,1,0:T(8,128)(2,1)S(1)}, u32[]{:S(2)}, u32[]{:S(2)}) async-start(bf16[32,8,2048]{2,1,0:T(8,128)(2,1)} %fusion), calls=%async_computation | async-start | bytes 2097152 | tf_op jit(solution)/shard_map/all_to_all | solution.py:529
  17.8 219.1 %all-gather.3.cloned.1.call-start = ((), (), s32[]{:S(2)}) async-start(), calls=%async_computation.2 | async-start | bytes 11796480 | tf_op jit(solution)/shard_map/all_gather | solution.py:684
  48.1 64.5 %collective-permute-start.3 = (bf16[768,1536]{1,0:T(8,128)(2,1)}, bf16[768,1536]{1,0:T(8,128)(2,1)}, u32[]{:S(2)}, u32[]{:S(2)}) collective-permute-start(bf16[768,1536]{1,0:T(8,128)(2,1)} %shard_map.218), channel_id=1, source_target_pairs={{0,8},{4,12},{8,16},{12,20},{16,24},{20,28},{24,0},{28,4},{1,9},{5... | collective-permute-start | bytes 7077896 | tf_op jit(solution)/shard_map/ppermute | solution.py:619
  50.8 9.3 %collective-permute-start = (bf16[256,2048]{1,0:T(8,128)(2,1)S(1)}, bf16[256,2048]{1,0:T(8,128)(2,1)}, u32[]{:S(2)}, u32[]{:S(2)}) collective-permute-start(bf16[256,2048]{1,0:T(8,128)(2,1)S(1)} %convolution_convert_fusion.2.refs_0_.refs_9_), channel_id=1, source_target_pairs={{0,1},{1,0},{2,3},{3,2},{4,5},{5,4},{6,7},{7,6},{8,9},{9,8},{10,11... | collective-permute-start | bytes 3145736 | tf_op jit(solution)/shard_map/ppermute | solution.py:23
  50.8 25.6 %collective-permute-start.1 = (bf16[256,2048]{1,0:T(8,128)(2,1)S(1)}, bf16[256,2048]{1,0:T(8,128)(2,1)S(1)}, u32[]{:S(2)}, u32[]{:S(2)}) collective-permute-start(bf16[256,2048]{1,0:T(8,128)(2,1)S(1)} %convolution_convert_fusion.2.refs_0_.refs_9_), channel_id=1, source_target_pairs={{0,2},{1,3},{2,0},{3,1},{4,6},{5,7},{6,4},{7,5},{8,10},{9,11},{10,... | collective-permute-start | bytes 3145736 | tf_op jit(solution)/shard_map/ppermute | solution.py:23
  77.4 6.8 %collective-permute-start.2 = (bf16[256,2048]{1,0:T(8,128)(2,1)}, bf16[256,2048]{1,0:T(8,128)(2,1)S(1)}, u32[]{:S(2)}, u32[]{:S(2)}) collective-permute-start(bf16[256,2048]{1,0:T(8,128)(2,1)} %shard_map.214.refs_0_), channel_id=1, source_target_pairs={{0,1},{1,0},{2,3},{3,2},{4,5},{5,4},{6,7},{7,6},{8,9},{9,8},{10,11... | collective-permute-start | bytes 3145736 | tf_op jit(solution)/shard_map/ppermute | solution.py:23
  116.1 25.5 %collective-permute-start.6 = (bf16[256,2048]{1,0:T(8,128)(2,1)S(1)}, bf16[256,2048]{1,0:T(8,128)(2,1)S(1)}, u32[]{:S(2)}, u32[]{:S(2)}) collective-permute-start(bf16[256,2048]{1,0:T(8,128)(2,1)S(1)} %add_convert_fusion.1.refs_13_), channel_id=1, source_target_pairs={{0,2},{1,3},{2,0},{3,1},{4,6},{5,7},{6,4},{7,5},{8,10},{9,11},{10,... | collective-permute-start | bytes 3145736 | tf_op jit(solution)/shard_map/ppermute | solution.py:23
  116.1 55.6 %collective-permute-start.9 = (bf16[768,1536]{1,0:T(8,128)(2,1)}, bf16[768,1536]{1,0:T(8,128)(2,1)S(1)}, u32[]{:S(2)}, u32[]{:S(2)}) collective-permute-start(bf16[768,1536]{1,0:T(8,128)(2,1)} %collective-permute-done.3.refs_1_), channel_id=1, source_target_pairs={{0,8},{4,12},{8,16},{12,20},{16,24},{20,28},{24,0},{28,4},{1,9},{5... | collective-permute-start | bytes 7077896 | tf_op jit(solution)/shard_map/ppermute | solution.py:619
  174.4 24.7 %collective-permute-start.10 = (bf16[256,2048]{1,0:T(8,128)(2,1)S(1)}, bf16[256,2048]{1,0:T(8,128)(2,1)}, u32[]{:S(2)}, u32[]{:S(2)}) collective-permute-start(bf16[256,2048]{1,0:T(8,128)(2,1)S(1)} %copy-done.5), channel_id=1, source_target_pairs={{0,4},{4,0},{8,12},{12,8},{16,20},{20,16},{24,28},{28,24},{1,5},{5... | collective-permute-start | bytes 3145736 | tf_op jit(solution)/shard_map/ppermute | solution.py:23
  174.4 24.7 %collective-permute-start.12 = (bf16[16,2048]{1,0:T(8,128)(2,1)S(1)}, bf16[16,2048]{1,0:T(8,128)(2,1)S(1)}, u32[]{:S(2)}, u32[]{:S(2)}) collective-permute-start(bf16[16,2048]{1,0:T(8,128)(2,1)S(1)} %copy-done.16), channel_id=1, source_target_pairs={{0,1},{1,0},{2,3},{3,2},{4,5},{5,4},{6,7},{7,6},{8,9},{9,8},{10,11... | collective-permute-start | bytes 196616 | tf_op jit(solution)/shard_map/ppermute | solution.py:23
  174.4 24.7 %collective-permute-start.13 = (bf16[16,2048]{1,0:T(8,128)(2,1)S(1)}, bf16[16,2048]{1,0:T(8,128)(2,1)S(1)}, u32[]{:S(2)}, u32[]{:S(2)}) collective-permute-start(bf16[16,2048]{1,0:T(8,128)(2,1)S(1)} %copy-done.16), channel_id=1, source_target_pairs={{0,2},{1,3},{2,0},{3,1},{4,6},{5,7},{6,4},{7,5},{8,10},{9,11},{10,... | collective-permute-start | bytes 196616 | tf_op jit(solution)/shard_map/ppermute | solution.py:23
  176.1 23.0 %collective-permute-start.14 = (bf16[16,2048]{1,0:T(8,128)(2,1)S(1)}, bf16[16,2048]{1,0:T(8,128)(2,1)S(1)}, u32[]{:S(2)}, u32[]{:S(2)}) collective-permute-start(bf16[16,2048]{1,0:T(8,128)(2,1)S(1)} %copy-done.16), channel_id=1, source_target_pairs={{0,3},{1,2},{2,1},{3,0},{4,7},{5,6},{6,5},{7,4},{8,11},{9,10},{10,... | collective-permute-start | bytes 196616 | tf_op jit(solution)/shard_map/ppermute | solution.py:23
  176.2 38.9 %collective-permute-start.18 = (bf16[256,2048]{1,0:T(8,128)(2,1)S(1)}, bf16[256,2048]{1,0:T(8,128)(2,1)}, u32[]{:S(2)}, u32[]{:S(2)}) collective-permute-start(bf16[256,2048]{1,0:T(8,128)(2,1)S(1)} %copy-done.5), channel_id=1, source_target_pairs={{0,8},{4,12},{8,0},{12,4},{16,24},{20,28},{24,16},{28,20},{1,9},{5... | collective-permute-start | bytes 3145736 | tf_op jit(solution)/shard_map/ppermute | solution.py:23
  199.1 27.8 %collective-permute-start.11 = (bf16[256,2048]{1,0:T(8,128)(2,1)}, bf16[256,2048]{1,0:T(8,128)(2,1)S(1)}, u32[]{:S(2)}, u32[]{:S(2)}) collective-permute-start(bf16[256,2048]{1,0:T(8,128)(2,1)} %collective-permute-done.10.refs_0_), channel_id=1, source_target_pairs={{0,8},{4,12},{8,0},{12,4},{16,24},{20,28},{24,16},{28,20},{1,9},{5... | collective-permute-start | bytes 3145736 | tf_op jit(solution)/shard_map/ppermute | solution.py:23
  200.7 25.6 %collective-permute-start.16 = (bf16[16,2048]{1,0:T(8,128)(2,1)S(1)}, bf16[16,2048]{1,0:T(8,128)(2,1)S(1)}, u32[]{:S(2)}, u32[]{:S(2)}) collective-permute-start(bf16[16,2048]{1,0:T(8,128)(2,1)S(1)} %fusion.15.refs_1_), channel_id=1, source_target_pairs={{0,8},{4,12},{8,0},{12,4},{16,24},{20,28},{24,16},{28,20},{1,9},{5... | collective-permute-start | bytes 196616 | tf_op jit(solution)/shard_map/ppermute | solution.py:23
  204.7 22.3 %collective-permute-start.17 = (bf16[16,2048]{1,0:T(8,128)(2,1)S(1)}, bf16[16,2048]{1,0:T(8,128)(2,1)S(1)}, u32[]{:S(2)}, u32[]{:S(2)}) collective-permute-start(bf16[16,2048]{1,0:T(8,128)(2,1)S(1)} %collective-permute-done.15.refs_6_.refs_2_), channel_id=1, source_target_pairs={{0,8},{4,12},{8,0},{12,4},{16,24},{20,28},{24,16},{28,20},{1,9},{5... | collective-permute-start | bytes 196616 | tf_op jit(solution)/shard_map/ppermute | solution.py:23
  248.2 26.8 %collective-permute-start.19 = (bf16[256,2048]{1,0:T(8,128)(2,1)}, bf16[256,2048]{1,0:T(8,128)(2,1)S(1)}, u32[]{:S(2)}, u32[]{:S(2)}) collective-permute-start(bf16[256,2048]{1,0:T(8,128)(2,1)} %get-tuple-element.67.refs_13_), channel_id=1, source_target_pairs={{0,4},{4,0},{8,12},{12,8},{16,20},{20,16},{24,28},{28,24},{1,5},{5... | collective-permute-start | bytes 3145736 | tf_op jit(solution)/shard_map/ppermute | solution.py:23
  250.2 36.9 %collective-permute-start.20 = (bf16[256,2048]{1,0:T(8,128)(2,1)}, bf16[256,2048]{1,0:T(8,128)(2,1)}, u32[]{:S(2)}, u32[]{:S(2)}) collective-permute-start(bf16[256,2048]{1,0:T(8,128)(2,1)} %get-tuple-element.69), channel_id=1, source_target_pairs={{0,8},{4,12},{8,0},{12,4},{16,24},{20,28},{24,16},{28,20},{1,9},{5... | collective-permute-start | bytes 3145736 | tf_op jit(solution)/shard_map/ppermute | solution.py:23
  259.6 43.2 %collective-permute-start.21 = (bf16[256,2048]{1,0:T(8,128)(2,1)}, bf16[256,2048]{1,0:T(8,128)(2,1)}, u32[]{:S(2)}, u32[]{:S(2)}) collective-permute-start(bf16[256,2048]{1,0:T(8,128)(2,1)} %get-tuple-element.68.refs_5_), channel_id=1, source_target_pairs={{0,12},{4,8},{8,4},{12,0},{16,28},{20,24},{24,20},{28,16},{1,13},{... | collective-permute-start | bytes 3145736 | tf_op jit(solution)/shard_map/ppermute | solution.py:23
  260.8 35.0 %collective-permute-start.22 = (bf16[16,2048]{1,0:T(8,128)(2,1)}, bf16[16,2048]{1,0:T(8,128)(2,1)S(1)}, u32[]{:S(2)}, u32[]{:S(2)}) collective-permute-start(bf16[16,2048]{1,0:T(8,128)(2,1)} %get-tuple-element.71), channel_id=1, source_target_pairs={{0,4},{4,0},{8,12},{12,8},{16,20},{20,16},{24,28},{28,24},{1,5},{5... | collective-permute-start | bytes 196616 | tf_op jit(solution)/shard_map/ppermute | solution.py:23
  262.8 36.6 %collective-permute-start.23 = (bf16[16,2048]{1,0:T(8,128)(2,1)}, bf16[16,2048]{1,0:T(8,128)(2,1)S(1)}, u32[]{:S(2)}, u32[]{:S(2)}) collective-permute-start(bf16[16,2048]{1,0:T(8,128)(2,1)} %get-tuple-element.72), channel_id=1, source_target_pairs={{0,8},{4,12},{8,0},{12,4},{16,24},{20,28},{24,16},{28,20},{1,9},{5... | collective-permute-start | bytes 196616 | tf_op jit(solution)/shard_map/ppermute | solution.py:23
  275.1 24.8 %collective-permute-start.24 = (bf16[16,2048]{1,0:T(8,128)(2,1)}, bf16[16,2048]{1,0:T(8,128)(2,1)S(1)}, u32[]{:S(2)}, u32[]{:S(2)}) collective-permute-start(bf16[16,2048]{1,0:T(8,128)(2,1)} %get-tuple-element.73), channel_id=1, source_target_pairs={{0,12},{4,8},{8,4},{12,0},{16,28},{20,24},{24,20},{28,16},{1,13},{... | collective-permute-start | bytes 196616 | tf_op jit(solution)/shard_map/ppermute | solution.py:23
  310.6 11.9 %collective-permute-start.27 = (bf16[64,2048]{1,0:T(8,128)(2,1)S(1)}, bf16[64,2048]{1,0:T(8,128)(2,1)S(1)}, u32[]{:S(2)}, u32[]{:S(2)}) collective-permute-start(bf16[64,2048]{1,0:T(8,128)(2,1)S(1)} %pad_maximum_fusion.4), channel_id=1, source_target_pairs={{0,16},{4,20},{8,24},{12,28},{16,0},{20,4},{24,8},{28,12},{1,17},{... | collective-permute-start | bytes 786440 | tf_op jit(solution)/shard_map/ppermute | solution.py:23
  313.0 37.0 %all-to-all-start.1 = ((bf16[32,8,2048]{2,1,0:T(8,128)(2,1)}), bf16[32,8,2048]{2,1,0:T(8,128)(2,1)S(1)}, u32[]{:S(2)}, u32[]{:S(2)}) async-start(bf16[32,8,2048]{2,1,0:T(8,128)(2,1)} %fusion.1), calls=%async_computation.1 | async-start | bytes 2097152 | tf_op jit(solution)/shard_map/all_to_all | solution.py:529
  (37 other events, 182.0 us)
Sparse Core Ops, SparseCore 0:
  173.3 61.6 all-gather.2
